TPU v7x, 32 devices: a whole 2x2x4 slice. The times are simulated.
32 devices in a mesh: gx: 2 (over x), gy: 4 (over y, core), gz: 4 (over z).
Axes of the slice: x: 2, y: 2, z: 4, core: 2. Of those that a mesh axis runs over, the one named last changes fastest.
Arguments:
- normed: bfloat16 [4096, 3072], P(('gy', 'gx'), 'gz'), may hold values from -6 to 6
- out_grad: bfloat16 [4096, 3072], P(('gy', 'gx'), 'gz'), may hold values from -6 to 6
- projected: bfloat16 [4096, 9216], P('gy', 'gx'), may hold values from -5 to 5
- mixed_heads: bfloat16 [4096, 3072], P('gy', 'gx'), may hold values from -6 to 6
- hidden_pre: bfloat16 [4096, 12288], P('gy', 'gx'), may hold values from -6 to 6
- attend_in: bfloat16 [3072, 9216], P('gz', ('gx', 'gy')), may hold values from -0.109375 to 0.109375
- hidden_in: bfloat16 [3072, 12288], P('gz', ('gx', 'gy')), may hold values from -0.109375 to 0.109375
- attend_out: bfloat16 [3072, 3072], P(('gx', 'gy'), 'gz'), may hold values from -0.109375 to 0.109375
- hidden_out: bfloat16 [12288, 3072], P(('gx', 'gy'), 'gz'), may hold values from -0.0546875 to 0.0546875
Outputs:
- normed_grad: bfloat16 [4096, 3072], P(('gy', 'gx'), 'gz')
- attend_in_grad: bfloat16 [3072, 9216], P('gz', ('gx', 'gy'))
- hidden_in_grad: bfloat16 [3072, 12288], P('gz', ('gx', 'gy'))
- attend_out_grad: bfloat16 [3072, 3072], P(('gx', 'gy'), 'gz')
- hidden_out_grad: bfloat16 [12288, 3072], P(('gx', 'gy'), 'gz')
All inputs are finite; a program needn't handle non-finite values.
Results may differ from a plain program's by a relative error of at most 0.02.
Values may be sent and summed in bfloat16 or wider, within the bound.
A program may use at most 256 MiB of HBM per device.

v0:
```python
import jax
import jax.numpy as jnp
from jax import lax
from jax.sharding import PartitionSpec as P

HEAD = 128
LEN = 1024


def gelu_value(values):
    return 0.5 * values * (1.0 + lax.erf(values * 0.7071067811865476))


def gelu_slope(values):
    return (
        0.5 * (1.0 + lax.erf(values * 0.7071067811865476))
        + values * jnp.exp(-0.5 * values * values) * 0.3989422804014327
    )


def local(
    normed,
    out_grad,
    projected,
    mixed_heads,
    hidden_pre,
    attend_in,
    hidden_in,
    attend_out,
    hidden_out,
):
    slab_count = projected.shape[0]
    depth = lax.axis_size("gz")
    block = slab_count // depth
    offset = lax.axis_index("gz") * block
    normed_slab, grad_slab = (
        lax.all_gather(normed, "gx", axis=0, tiled=True),
        lax.all_gather(out_grad, "gx", axis=0, tiled=True),
    )
    attend_cols, hidden_cols, attend_rows, hidden_rows = (
        lax.all_gather(attend_in, "gy", axis=1, tiled=True),
        lax.all_gather(hidden_in, "gy", axis=1, tiled=True),
        lax.all_gather(attend_out, "gy", axis=0, tiled=True),
        lax.all_gather(hidden_out, "gy", axis=0, tiled=True),
    )
    merge_part = jnp.einsum("td,gd->tg", grad_slab, attend_rows, preferred_element_type=jnp.float32)
    hidden_part = jnp.einsum(
        "td,gd->tg", grad_slab, hidden_rows, preferred_element_type=jnp.float32
    )
    pre_float = hidden_pre.astype(jnp.float32)
    merge_rows, hidden_sum = (
        lax.psum_scatter(merge_part, "gz", scatter_dimension=0, tiled=True),
        lax.psum_scatter(hidden_part, "gz", scatter_dimension=0, tiled=True),
    )
    slope_rows = gelu_slope(lax.dynamic_slice_in_dim(pre_float, offset, block, 0))
    hidden_grad_rows = (hidden_sum * slope_rows).astype(jnp.bfloat16)
    heads_grad = merge_rows.astype(jnp.bfloat16)
    heads_here = projected.shape[1] // (3 * HEAD)
    score_scale = HEAD ** (-0.5)
    span = max(block, LEN)
    keyed = projected.reshape(slab_count, heads_here, 3, HEAD)
    local_rows = lax.dynamic_slice_in_dim(keyed, offset, block, 0)
    queries = local_rows[:, :, 0]
    key_rows = keyed[:, :, 1]
    value_rows = keyed[:, :, 2]
    head_grad = heads_grad.reshape(block, heads_here, HEAD)
    scores = (
        jnp.einsum("qhd,khd->hqk", queries, key_rows, preferred_element_type=jnp.float32)
        * score_scale
    )
    largest = jnp.max(scores, axis=2, keepdims=True)
    weights = jnp.exp(scores - largest)
    probability = weights / jnp.sum(weights, axis=2, keepdims=True)
    value_grad = jnp.einsum(
        "hqk,qhd->khd",
        probability.astype(jnp.bfloat16),
        head_grad,
        preferred_element_type=jnp.float32,
    )
    prob_grad = jnp.einsum(
        "qhd,khd->hqk", head_grad, value_rows, preferred_element_type=jnp.float32
    )
    centre = jnp.sum(probability * prob_grad, axis=2, keepdims=True)
    score_grad = (probability * (prob_grad - centre)).astype(jnp.bfloat16)
    query_grad = score_scale * jnp.einsum(
        "hqk,khd->qhd", score_grad, key_rows, preferred_element_type=jnp.float32
    )
    key_grad = score_scale * jnp.einsum(
        "hqk,qhd->khd", score_grad, queries, preferred_element_type=jnp.float32
    )
    key_value = jnp.stack([key_grad, value_grad], axis=2).reshape(span, heads_here * 2 * HEAD)
    summed = (
        lax.psum_scatter(key_value.astype(jnp.bfloat16), "gz", scatter_dimension=0, tiled=True)
        .astype(jnp.float32)
        .reshape(block, heads_here, 2, HEAD)
    )
    projected_grad_rows = (
        jnp.concatenate([query_grad[:, :, None], summed], axis=2)
        .reshape(block, 3 * heads_here * HEAD)
        .astype(jnp.bfloat16)
    )
    projected_grad, hidden_grad = (
        lax.all_gather(projected_grad_rows, "gz", axis=0, tiled=True),
        lax.all_gather(hidden_grad_rows, "gz", axis=0, tiled=True),
    )
    local_grad = jnp.einsum(
        "tq,dq->td", projected_grad, attend_cols, preferred_element_type=jnp.float32
    ) + jnp.einsum("tq,dq->td", hidden_grad, hidden_cols, preferred_element_type=jnp.float32)
    normed_grad = lax.psum_scatter(
        local_grad.astype(jnp.bfloat16), "gx", scatter_dimension=0, tiled=True
    )
    activated = gelu_value(pre_float).astype(jnp.bfloat16)
    part_attend_in = jnp.einsum(
        "td,tq->dq", normed_slab, projected_grad, preferred_element_type=jnp.float32
    )
    part_hidden_in = jnp.einsum(
        "td,tq->dq", normed_slab, hidden_grad, preferred_element_type=jnp.float32
    )
    part_attend_out = jnp.einsum(
        "tg,td->gd", mixed_heads, grad_slab, preferred_element_type=jnp.float32
    )
    part_hidden_out = jnp.einsum(
        "tg,td->gd", activated, grad_slab, preferred_element_type=jnp.float32
    )
    sum_attend_in, sum_hidden_in, sum_attend_out, sum_hidden_out = (
        lax.psum_scatter(
            part_attend_in.astype(jnp.bfloat16), "gy", scatter_dimension=1, tiled=True
        ).astype(jnp.float32),
        lax.psum_scatter(
            part_hidden_in.astype(jnp.bfloat16), "gy", scatter_dimension=1, tiled=True
        ).astype(jnp.float32),
        lax.psum_scatter(
            part_attend_out.astype(jnp.bfloat16), "gy", scatter_dimension=0, tiled=True
        ).astype(jnp.float32),
        lax.psum_scatter(
            part_hidden_out.astype(jnp.bfloat16), "gy", scatter_dimension=0, tiled=True
        ).astype(jnp.float32),
    )
    return (
        normed_grad,
        sum_attend_in.astype(jnp.bfloat16),
        sum_hidden_in.astype(jnp.bfloat16),
        sum_attend_out.astype(jnp.bfloat16),
        sum_hidden_out.astype(jnp.bfloat16),
    )


def solution(mesh):
    placed = (
        P(("gy", "gx"), "gz"),
        P(("gy", "gx"), "gz"),
        P("gy", "gx"),
        P("gy", "gx"),
        P("gy", "gx"),
        P("gz", ("gx", "gy")),
        P("gz", ("gx", "gy")),
        P(("gx", "gy"), "gz"),
        P(("gx", "gy"), "gz"),
    )
    return jax.shard_map(
        local,
        mesh=mesh,
        in_specs=placed,
        out_specs=(
            P(("gy", "gx"), "gz"),
            P("gz", ("gx", "gy")),
            P("gz", ("gx", "gy")),
            P(("gx", "gy"), "gz"),
            P(("gx", "gy"), "gz"),
        ),
        check_vma=False,
    )
```

profile of v0, /device:TPU:4, one launch (start us, length us, event | category | flops | bytes accessed | tf_op | source)
XLA Modules:
  0.0 1612.5 jit_solution(10149110505384659074)
XLA Ops:
  8.7 29.3 %all-gather.9.cloned.1.call-done = bf16[1024,768]{1,0:T(8,128)(2,1)} async-done(((bf16[512,768]{1,0:T(8,128)(2,1)}), bf16[1024,768]{1,0:T(8,128)(2,1)}) %all-gather.9.cloned.1.call-update) | async-done | bytes 1572880 | tf_op jit(solution)/shard_map/all_gather | solution.py:38
  38.0 24.5 %all-gather.11.cloned.1.call-done = bf16[1536,768]{1,0:T(8,128)(2,1)} async-done(((bf16[384,768]{1,0:T(8,128)(2,1)}), bf16[1536,768]{1,0:T(8,128)(2,1)}) %all-gather.11.cloned.1.call-update) | async-done | bytes 2359312 | tf_op jit(solution)/shard_map/all_gather | solution.py:43
  62.5 7.4 fusion.36
  70.5 12.5 copy.21
  83.0 8.5 fusion.21
  91.5 16.0 fusion.35
  107.5 74.5 %reduce-scatter.9.cloned.1.call-done = f32[256,1536]{1,0:T(8,128)} async-done(((f32[1024,1536]{1,0:T(8,128)}), f32[256,1536]{1,0:T(8,128)}) %reduce-scatter.9.cloned.1.call-update) | async-done | bytes 1572880 | tf_op jit(solution)/shard_map/reduce_scatter | solution.py:52
  186.6 18.7 %convert_bitcast_fusion = bf16[1024,12,1,128]{0,3,1,2:T(8,128)(2,1)} fusion(bf16[256,12,128]{0,2,1:T(8,128)(2,1)} %bitcast.73, f32[12,256]{1,0:T(8,128)S(1)} %get-tuple-element.15, f32[12,256,1024]{2,1,0:T(8,128)} %fusion.21), kind=kOutput, calls=%fused_computation.33 | convolution fusion | flops 822611968 | bytes 16527360 | tf_op jit(solution)/shard_map/hqk,qhd->khd/dot_general | solution.py:74
  205.4 11.6 multiply_reduce_fusion
  219.2 6.2 multiply_convert_fusion.1
  234.5 12.5 all-gather.17.cloned.1.call-done
  247.0 17.6 %fusion.38 = f32[1024,6144]{1,0:T(8,128)} fusion(bf16[1024,768]{1,0:T(8,128)(2,1)} %all-gather.9.cloned.1.call-done, bf16[6144,768]{1,0:T(8,128)(2,1)} %all-gather.17.cloned.1.call-done), kind=kOutput, calls=%fused_computation.49 | convolution fusion | flops 9663676416 | bytes 36175872 | tf_op jit(solution)/shard_map/td,gd->tg/dot_general | solution.py:47
  265.5 6.9 fusion.24
  272.4 88.8 %reduce-scatter.11.cloned.1.call-done = bf16[256,3072]{0,1:T(8,128)(2,1)} async-done(((bf16[1024,3072]{0,1:T(8,128)(2,1)}), bf16[256,3072]{0,1:T(8,128)(2,1)}) %reduce-scatter.11.cloned.1.call-update) | async-done | bytes 1572880 | tf_op jit(solution)/shard_map/reduce_scatter | solution.py:93
  364.4 14.6 convert_element_type.61
  379.0 399.3 %reduce-scatter.13.cloned.1.call-done = f32[256,6144]{1,0:T(8,128)} async-done(((f32[1024,6144]{1,0:T(8,128)}), f32[256,6144]{1,0:T(8,128)}) %reduce-scatter.13.cloned.1.call-update) | async-done | bytes 6291472 | tf_op jit(solution)/shard_map/reduce_scatter | solution.py:53
  778.3 8.0 fusion.13
  787.7 21.3 %all-gather.23.cloned.1.call-done = bf16[1024,768]{1,0:T(8,128)(2,1)} async-done(((bf16[512,768]{1,0:T(8,128)(2,1)}), bf16[1024,768]{1,0:T(8,128)(2,1)}) %all-gather.23.cloned.1.call-update) | async-done | bytes 1572880 | tf_op jit(solution)/shard_map/all_gather | solution.py:37
  808.9 168.5 %all-gather.13.cloned.1.call-done = bf16[1024,4608]{0,1:T(8,128)(2,1)} async-done(((bf16[256,4608]{0,1:T(8,128)(2,1)}), bf16[1024,4608]{0,1:T(8,128)(2,1)}) %all-gather.13.cloned.1.call-update) | async-done | bytes 9437200 | tf_op jit(solution)/shard_map/all_gather | solution.py:103
  977.4 12.8 fusion.7
  990.3 205.2 %all-gather.19.cloned.1.call-done = bf16[1024,6144]{1,0:T(8,128)(2,1)} async-done(((bf16[256,6144]{1,0:T(8,128)(2,1)}), bf16[1024,6144]{1,0:T(8,128)(2,1)}) %all-gather.19.cloned.1.call-update) | async-done | bytes 12582928 | tf_op jit(solution)/shard_map/all_gather | solution.py:104
  1195.5 15.8 fusion.4
  1216.9 16.8 %fusion.3 = bf16[6144,768]{1,0:T(8,128)(2,1)} fusion(bf16[1024,768]{1,0:T(8,128)(2,1)} %all-gather.9.cloned.1.call-done, bf16[1024,6144]{1,0:T(8,128)(2,1)} %param.13), kind=kOutput, calls=%fused_computation.8 | convolution fusion | flops 9706143744 | bytes 23592960 | tf_op jit(solution)/shard_map/tg,td->gd/dot_general | solution.py:122
  1233.8 11.1 all-gather.15.cloned.1.call-done
  1244.9 13.4 fusion.37
  1258.3 52.6 %all-gather.21.cloned.1.call-done = bf16[768,6144]{1,0:T(8,128)(2,1)} async-done(((bf16[768,1536]{1,0:T(8,128)(2,1)}), bf16[768,6144]{1,0:T(8,128)(2,1)}) %all-gather.21.cloned.1.call-update) | async-done | bytes 9437200 | tf_op jit(solution)/shard_map/all_gather | solution.py:42
  1310.8 17.0 %add_convert_fusion = bf16[1024,768]{1,0:T(8,128)(2,1)} fusion(f32[1024,768]{1,0:T(8,128)} %fusion.37, bf16[1024,6144]{1,0:T(8,128)(2,1)} %all-gather.19.cloned.1.call-done, bf16[768,6144]{1,0:T(8,128)(2,1)} %all-gather.21.cloned.1.call-done), kind=kOutput, calls=%fused_computation.32 | convolution fusion | flops 9665249280 | bytes 26738688 | tf_op jit(solution)/shard_map/tq,dq->td/dot_general | solution.py:108
  1327.8 49.2 %reduce-scatter.17.cloned.1.call-done = bf16[768,1152]{0,1:T(8,128)(2,1)} async-done(((bf16[768,4608]{0,1:T(8,128)(2,1)}), bf16[768,1152]{0,1:T(8,128)(2,1)}) %reduce-scatter.17.cloned.1.call-update) | async-done | bytes 1769488 | tf_op jit(solution)/shard_map/reduce_scatter | solution.py:126
  1380.9 77.2 %reduce-scatter.19.cloned.1.call-done = bf16[768,1536]{0,1:T(8,128)(2,1)} async-done(((bf16[768,6144]{0,1:T(8,128)(2,1)}), bf16[768,1536]{0,1:T(8,128)(2,1)}) %reduce-scatter.19.cloned.1.call-update) | async-done | bytes 2359312 | tf_op jit(solution)/shard_map/reduce_scatter | solution.py:129
  1462.3 31.8 %reduce-scatter.21.cloned.1.call-done = bf16[384,768]{1,0:T(8,128)(2,1)} async-done(((bf16[1536,768]{1,0:T(8,128)(2,1)}), bf16[384,768]{1,0:T(8,128)(2,1)}) %reduce-scatter.21.cloned.1.call-update) | async-done | bytes 589840 | tf_op jit(solution)/shard_map/reduce_scatter | solution.py:132
  1494.1 81.6 %reduce-scatter.23.cloned.1.call-done = bf16[1536,768]{1,0:T(8,128)(2,1)} async-done(((bf16[6144,768]{1,0:T(8,128)(2,1)}), bf16[1536,768]{1,0:T(8,128)(2,1)}) %reduce-scatter.23.cloned.1.call-update) | async-done | bytes 2359312 | tf_op jit(solution)/shard_map/reduce_scatter | solution.py:135
  1575.8 30.0 %reduce-scatter.15.cloned.1.call-done = bf16[512,768]{1,0:T(8,128)(2,1)} async-done(((bf16[1024,768]{1,0:T(8,128)(2,1)}), bf16[512,768]{1,0:T(8,128)(2,1)}) %reduce-scatter.15.cloned.1.call-update) | async-done | bytes 786448 | tf_op jit(solution)/shard_map/reduce_scatter | solution.py:109
  (54 shorter events, 37.2 us)
Async XLA Ops:
  7.2 1204.3 %copy-start = (bf16[1024,1536]{1,0:T(8,128)(2,1)S(1)}, bf16[1024,1536]{1,0:T(8,128)(2,1)}, u32[]{:S(2)}) copy-start(bf16[1024,1536]{1,0:T(8,128)(2,1)} %param.12) | copy-start | bytes 9437188
  7.2 30.8 %all-gather.9.cloned.1.call-start = ((), (), s32[]{:S(2)}) async-start(), calls=%async_computation.8 | async-start | bytes 2359296 | tf_op jit(solution)/shard_map/all_gather | solution.py:38
  7.9 54.6 %all-gather.11.cloned.1.call-start = ((), (), s32[]{:S(2)}) async-start(), calls=%async_computation.9 | async-start | bytes 2949120 | tf_op jit(solution)/shard_map/all_gather | solution.py:43
  8.7 173.3 %reduce-scatter.9.cloned.1.call-start = ((), (), s32[]{:S(2)}) async-start(), calls=%async_computation.10 | async-start | bytes 7864320 | tf_op jit(solution)/shard_map/reduce_scatter | solution.py:52
  69.9 177.1 %all-gather.17.cloned.1.call-start = ((), (), s32[]{:S(2)}) async-start(), calls=%async_computation.14 | async-start | bytes 11796480 | tf_op jit(solution)/shard_map/all_gather | solution.py:44
  70.5 290.6 %reduce-scatter.11.cloned.1.call-start = ((), (), s32[]{:S(2)}) async-start(), calls=%async_computation.11 | async-start | bytes 7864320 | tf_op jit(solution)/shard_map/reduce_scatter | solution.py:93
  205.4 11.6 slice-start
  205.4 12.7 slice-start.1
  205.4 13.8 slice-start.2
  225.4 2.6 copy-start.1
  228.0 2.5 copy-start.2
  234.5 543.8 %reduce-scatter.13.cloned.1.call-start = ((), (), s32[]{:S(2)}) async-start(), calls=%async_computation.15 | async-start | bytes 31457280 | tf_op jit(solution)/shard_map/reduce_scatter | solution.py:53
  264.7 544.3 %all-gather.23.cloned.1.call-start = ((), (), s32[]{:S(2)}) async-start(), calls=%async_computation.19 | async-start | bytes 2359296 | tf_op jit(solution)/shard_map/all_gather | solution.py:37
  265.4 712.0 %all-gather.13.cloned.1.call-start = ((), (), s32[]{:S(2)}) async-start(), calls=%async_computation.12 | async-start | bytes 11796480 | tf_op jit(solution)/shard_map/all_gather | solution.py:103
  364.4 831.2 %all-gather.19.cloned.1.call-start = ((), (), s32[]{:S(2)}) async-start(), calls=%async_computation.16 | async-start | bytes 15728640 | tf_op jit(solution)/shard_map/all_gather | solution.py:104
  786.3 458.6 %all-gather.15.cloned.1.call-start = ((), (), s32[]{:S(2)}) async-start(), calls=%async_computation.13 | async-start | bytes 8847360 | tf_op jit(solution)/shard_map/all_gather | solution.py:41
  786.9 523.9 %all-gather.21.cloned.1.call-start = ((), (), s32[]{:S(2)}) async-start(), calls=%async_computation.17 | async-start | bytes 11796480 | tf_op jit(solution)/shard_map/all_gather | solution.py:42
  787.6 589.4 %reduce-scatter.17.cloned.1.call-start = ((), (), s32[]{:S(2)}) async-start(), calls=%async_computation.20 | async-start | bytes 8847360 | tf_op jit(solution)/shard_map/reduce_scatter | solution.py:126
  990.3 467.7 %reduce-scatter.19.cloned.1.call-start = ((), (), s32[]{:S(2)}) async-start(), calls=%async_computation.21 | async-start | bytes 11796480 | tf_op jit(solution)/shard_map/reduce_scatter | solution.py:129
  1211.4 282.7 %reduce-scatter.21.cloned.1.call-start = ((), (), s32[]{:S(2)}) async-start(), calls=%async_computation.22 | async-start | bytes 2949120 | tf_op jit(solution)/shard_map/reduce_scatter | solution.py:132
  1216.8 358.9 %reduce-scatter.23.cloned.1.call-start = ((), (), s32[]{:S(2)}) async-start(), calls=%async_computation.23 | async-start | bytes 11796480 | tf_op jit(solution)/shard_map/reduce_scatter | solution.py:135
  1233.7 372.0 %reduce-scatter.15.cloned.1.call-start = ((), (), s32[]{:S(2)}) async-start(), calls=%async_computation.18 | async-start | bytes 2359296 | tf_op jit(solution)/shard_map/reduce_scatter | solution.py:109
Sparse Core Ops, SparseCore 0:
  9.6 28.4 all-gather.8
  39.6 22.9 all-gather.10
  70.0 111.9 reduce-scatter.8
  183.4 63.5 all-gather.16
  249.2 111.9 reduce-scatter.10
  363.3 414.8 reduce-scatter.12
  779.9 28.9 all-gather.22
  811.1 166.2 all-gather.12
  979.1 216.3 all-gather.18
  1197.0 47.8 all-gather.14
  1246.5 64.2 all-gather.20
  1313.4 63.5 reduce-scatter.16
  1379.6 78.3 reduce-scatter.18
  1461.0 33.0 reduce-scatter.20
  1497.3 78.3 reduce-scatter.22
  1578.5 27.2 reduce-scatter.14
where the time goes:
time: 1620 us; the launch traced here: 1610 us
  waiting for transfers between devices  1360 us (84%)
  matrix products  154 us (10%)
  other arithmetic  51 us (3%)
  local copies, waits for them, and re-layouts  31 us (2%)
    reduce_scatter x1, waiting for transfers between devices, local(): lax.psum_scatter(hidden_part, 'gz', scatter_dimension=0, tiled=True)  399 us
    all_gather x1, waiting for transfers between devices, local(): lax.all_gather(hidden_grad_rows, 'gz', axis=0, tiled=True)  205 us
    all_gather x1, waiting for transfers between devices, local(): lax.all_gather(projected_grad_rows, 'gz', axis=0, tiled=True)  169 us
    reduce_scatter x1, waiting for transfers between devices, local(): lax.psum_scatter(key_value.astype(jnp.bfloat16), 'gz', scatter_dimension=...  88.8 us
    reduce_scatter x1, waiting for transfers between devices, local(): lax.psum_scatter(part_hidden_out.astype(jnp.bfloat16), 'gy', scatter_dime...  81.6 us
    reduce_scatter x1, waiting for transfers between devices, local(): lax.psum_scatter(part_hidden_in.astype(jnp.bfloat16), 'gy', scatter_dimen...  77.2 us
    reduce_scatter x1, waiting for transfers between devices, local(): lax.psum_scatter(merge_part, 'gz', scatter_dimension=0, tiled=True)  74.5 us
    all_gather x1, waiting for transfers between devices, local(): lax.all_gather(hidden_in, 'gy', axis=1, tiled=True)  52.6 us
  transfers between devices with their start and end apart: 16, of which 16 were waited for; matrix products, arithmetic and copies ran while one was open for 14% of the time, Pallas kernels for 0%

commit v1 on v0

--- a/solution.py
+++ b/solution.py
@@ -1,6 +1,8 @@
 import jax
 import jax.numpy as jnp
 from jax import lax
+from jax.experimental import pallas as pl
+from jax.experimental.pallas import tpu as pltpu
 from jax.sharding import PartitionSpec as P
 
 HEAD = 128
@@ -145,6 +147,189 @@
     )
 
 
+SWAP = (0, 2, 1, 3)
+
+
+def attention_kernel(keyed_ref, grad_ref, out_ref):
+    score_scale = HEAD ** (-0.5)
+    across = (((1,), (1,)), ((), ()))
+    along = (((0,), (0,)), ((), ()))
+    keys = keyed_ref[:, HEAD : 2 * HEAD]
+    values = keyed_ref[:, 2 * HEAD :]
+    count = keyed_ref.shape[0]
+    step = min(256, count)
+    key_grad = jnp.zeros((count, HEAD), jnp.float32)
+    value_grad = jnp.zeros((count, HEAD), jnp.float32)
+    for start in range(0, count, step):
+        rows = slice(start, start + step)
+        queries = keyed_ref[rows, :HEAD]
+        grads = grad_ref[rows, :]
+        scores = (
+            lax.dot_general(queries, keys, across, preferred_element_type=jnp.float32)
+            * score_scale
+        )
+        weights = jnp.exp(scores - jnp.max(scores, axis=1, keepdims=True))
+        probability = weights / jnp.sum(weights, axis=1, keepdims=True)
+        prob_grad = lax.dot_general(grads, values, across, preferred_element_type=jnp.float32)
+        centre = jnp.sum(probability * prob_grad, axis=1, keepdims=True)
+        score_grad = (probability * (prob_grad - centre)).astype(jnp.bfloat16)
+        query_grad = score_scale * jnp.dot(score_grad, keys, preferred_element_type=jnp.float32)
+        out_ref[rows, :HEAD] = query_grad.astype(jnp.bfloat16)
+        key_grad += lax.dot_general(
+            score_grad, queries, along, preferred_element_type=jnp.float32
+        )
+        value_grad += lax.dot_general(
+            probability.astype(jnp.bfloat16), grads, along, preferred_element_type=jnp.float32
+        )
+    out_ref[:, HEAD : 2 * HEAD] = (score_scale * key_grad).astype(jnp.bfloat16)
+    out_ref[:, 2 * HEAD :] = value_grad.astype(jnp.bfloat16)
+
+
+def attention_backward(keyed, head_grad):
+    count = keyed.shape[0]
+    heads = keyed.shape[1] // (3 * HEAD)
+    return pl.pallas_call(
+        attention_kernel,
+        grid=(heads,),
+        in_specs=[
+            pl.BlockSpec((count, 3 * HEAD), lambda head: (0, head)),
+            pl.BlockSpec((count, HEAD), lambda head: (0, head)),
+        ],
+        out_specs=pl.BlockSpec((count, 3 * HEAD), lambda head: (0, head)),
+        out_shape=jax.ShapeDtypeStruct(keyed.shape, jnp.bfloat16),
+        compiler_params=pltpu.CompilerParams(vmem_limit_bytes=40 * 1024 * 1024),
+        cost_estimate=pl.CostEstimate(
+            flops=10 * heads * count * count * HEAD,
+            bytes_accessed=14 * heads * count * HEAD,
+            transcendentals=heads * count * count,
+        ),
+    )(keyed, head_grad)
+
+
+def exchange(block, axis, flip):
+    size = lax.axis_size(axis)
+    return lax.ppermute(block, axis, [(i, i ^ flip) for i in range(size)])
+
+
+def turn(block):
+    pairs = [
+        (g * 4 + z, SWAP[z] * 4 + SWAP[g]) for g in range(4) for z in range(4)
+    ]
+    return lax.ppermute(block, ("gy", "gz"), pairs)
+
+
+def gather_width(block, dim):
+    place = lax.axis_index("gy")
+    width = block.shape[dim]
+    shape = list(block.shape)
+    shape[dim] = 4 * width
+    whole = jnp.zeros(tuple(shape), block.dtype)
+    beside = exchange(block, "gy", 1)
+    opposite = exchange(block, "gy", 2)
+    last = exchange(opposite, "gy", 1)
+    for flip, part in ((0, block), (1, beside), (2, opposite), (3, last)):
+        whole = lax.dynamic_update_slice_in_dim(
+            whole, part, lax.bitwise_xor(place, flip) * width, dim
+        )
+    return whole
+
+
+def both_halves(half):
+    other = exchange(half, "gx", 1)
+    first = lax.axis_index("gx") == 0
+    return jnp.concatenate([jnp.where(first, half, other), jnp.where(first, other, half)], axis=0)
+
+
+def whole_width(rows):
+    blocks = lax.all_gather(rows, "gz", axis=0)
+    return jnp.concatenate([blocks[SWAP[i]] for i in range(4)], axis=1)
+
+
+def local_columns(
+    normed,
+    out_grad,
+    projected,
+    mixed_heads,
+    hidden_pre,
+    attend_in,
+    hidden_in,
+    attend_out,
+    hidden_out,
+):
+    side = lax.axis_index("gx")
+    deep = lax.axis_index("gz")
+    column = 2 * lax.rem(deep, 2) + deep // 2
+    half = normed.shape[0]
+    grad_own = both_halves(out_grad)
+    grad_slab = both_halves(whole_width(out_grad))
+    attend_rows = gather_width(turn(attend_out), 1)
+    hidden_rows = gather_width(turn(hidden_out), 1)
+    normed_slab = both_halves(whole_width(normed))
+    attend_cols = gather_width(turn(attend_in), 0)
+    hidden_cols = gather_width(turn(hidden_in), 0)
+
+    activated = gelu_value(hidden_pre.astype(jnp.float32)).astype(jnp.bfloat16)
+    part_attend_out = jnp.einsum(
+        "tg,td->gd", mixed_heads, grad_own, preferred_element_type=jnp.float32
+    ).astype(jnp.bfloat16)
+    part_hidden_out = jnp.einsum(
+        "tg,td->gd", activated, grad_own, preferred_element_type=jnp.float32
+    ).astype(jnp.bfloat16)
+    attend_out_grad = lax.psum_scatter(part_attend_out, "gy", scatter_dimension=0, tiled=True)
+    hidden_out_grad = lax.psum_scatter(part_hidden_out, "gy", scatter_dimension=0, tiled=True)
+
+    head_grad = jnp.einsum(
+        "td,gd->tg", grad_slab, attend_rows, preferred_element_type=jnp.float32
+    ).astype(jnp.bfloat16)
+    width = attend_in.shape[1]
+    keyed = lax.dynamic_slice_in_dim(projected, column * width, width, 1)
+    projected_grad = attention_backward(keyed, head_grad)
+
+    units = hidden_in.shape[1]
+    pre_here = lax.dynamic_slice_in_dim(hidden_pre, column * units, units, 1)
+    hidden_part = jnp.einsum(
+        "td,gd->tg", grad_slab, hidden_rows, preferred_element_type=jnp.float32
+    )
+    hidden_grad = (hidden_part * gelu_slope(pre_here.astype(jnp.float32))).astype(jnp.bfloat16)
+
+    part_attend_in = jnp.einsum(
+        "td,tq->dq", normed_slab, projected_grad, preferred_element_type=jnp.float32
+    ).astype(jnp.bfloat16)
+    part_hidden_in = jnp.einsum(
+        "td,tq->dq", normed_slab, hidden_grad, preferred_element_type=jnp.float32
+    ).astype(jnp.bfloat16)
+    attend_in_grad = turn(lax.psum_scatter(part_attend_in, "gy", scatter_dimension=0, tiled=True))
+    hidden_in_grad = turn(lax.psum_scatter(part_hidden_in, "gy", scatter_dimension=0, tiled=True))
+
+    def input_grad(start):
+        attend_part = lax.dynamic_slice_in_dim(projected_grad, start, half, 0)
+        hidden_part = lax.dynamic_slice_in_dim(hidden_grad, start, half, 0)
+        return jnp.einsum(
+            "tq,dq->td", attend_part, attend_cols, preferred_element_type=jnp.float32
+        ) + jnp.einsum("tq,dq->td", hidden_part, hidden_cols, preferred_element_type=jnp.float32)
+
+    arrived = exchange(input_grad((1 - side) * half).astype(jnp.bfloat16), "gx", 1)
+    row_grad = (input_grad(side * half) + arrived.astype(jnp.float32)).astype(jnp.bfloat16)
+    block = normed.shape[1]
+    row_grad = jnp.concatenate(
+        [row_grad[:, SWAP[i] * block : (SWAP[i] + 1) * block] for i in range(4)], axis=1
+    )
+    normed_grad = lax.psum_scatter(row_grad, "gz", scatter_dimension=1, tiled=True)
+    return normed_grad, attend_in_grad, hidden_in_grad, attend_out_grad, hidden_out_grad
+
+
+def chosen(*arrays):
+    normed, projected, attend_in = arrays[0], arrays[2], arrays[5]
+    sizes = tuple(lax.axis_size(axis) for axis in ("gx", "gy", "gz"))
+    fits = (
+        sizes == (2, 4, 4)
+        and projected.shape[0] == LEN
+        and attend_in.shape[1] % (3 * HEAD) == 0
+        and normed.shape[0] * 2 == LEN
+    )
+    return (local_columns if fits else local)(*arrays)
+
+
 def solution(mesh):
     placed = (
         P(("gy", "gx"), "gz"),
@@ -158,7 +343,7 @@
         P(("gx", "gy"), "gz"),
     )
     return jax.shard_map(
-        local,
+        chosen,
         mesh=mesh,
         in_specs=placed,
         out_specs=(

time: 1620 us -> 1010 us (0.62)
  waiting for transfers between devices: 1360 us -> 753 us
  matrix products: 154 us -> 99.4 us
  local copies, waits for them, and re-layouts: 31 us -> 63.9 us
  other arithmetic: 51 us -> 22.1 us
  starting transfers between devices: 0.64 us -> 26.5 us
    reduce_scatter x8 -> x4, waiting for transfers between devices: 832 us -> 51.9 us  [the longest x1 51.8 us: local_columns(): lax.psum_scatter(part_hidden_out, 'gy', scatter_dimension=0, tiled=True)]
    ppermute x0 -> x22, waiting for transfers between devices: none -> 697 us  [the longest x6 451 us: turn(): return lax.ppermute(block, ('gy', 'gz'), pairs)]
    all_gather x8 -> x2, waiting for transfers between devices: 525 us -> 2.5 us  [whole_width(): blocks = lax.all_gather(rows, 'gz', axis=0)]
    dot_general x13 -> x10, matrix products: 154 us -> 99.4 us  [the longest x1 18.2 us: local_columns(): jnp.einsum('td,gd->tg', grad_slab, hidden_rows, preferred_element_type=jn...]
    dynamic_update_slice x0 -> x16, local copies, waits for them, and re-layouts: none -> 33.3 us  [gather_width(): lax.dynamic_update_slice_in_dim(whole, part, lax.bitwise_xor(place, flip)...]
    ppermute x0 -> x22, starting transfers between devices: none -> 26 us  [the longest x6 19.4 us: turn(): return lax.ppermute(block, ('gy', 'gz'), pairs)]
    convert_element_type x4 -> x1, other arithmetic: 31.1 us -> 5.5 us  [local_columns(): (input_grad(side * half) + arrived.astype(jnp.float32)).astype(jnp.bfloat16)]
  transfers between devices with their start and end apart: 16 -> 29, of which waited for: 16 -> 14; matrix products, arithmetic and copies ran while one was open for 14% -> 16% of each run, Pallas kernels for 0% -> 1%
where the time goes in v1:
time: 1010 us; the launch traced here: 994 us
  waiting for transfers between devices  753 us (75%)
  matrix products  99.4 us (10%)
  local copies, waits for them, and re-layouts  63.9 us (6%)
  starting transfers between devices  26.5 us (3%)
  other arithmetic  22.1 us (2%)
  between operations  15 us (1%)
  Pallas kernels  14.1 us (1%)
    ppermute x6, waiting for transfers between devices, turn(): return lax.ppermute(block, ('gy', 'gz'), pairs)  451 us
    ppermute x16, waiting for transfers between devices, exchange(): return lax.ppermute(block, axis, [(i, i ^ flip) for i in range(size)])  247 us
    reduce_scatter x1, waiting for transfers between devices, local_columns(): lax.psum_scatter(part_hidden_out, 'gy', scatter_dimension=0, tiled=True)  51.8 us
    dynamic_update_slice x16, local copies, waits for them, and re-layouts, gather_width(): lax.dynamic_update_slice_in_dim(whole, part, lax.bitwise_xor(place, flip)...  33.3 us
  transfers between devices with their start and end apart: 29, of which 14 were waited for; matrix products, arithmetic and copies ran while one was open for 16% of the time, Pallas kernels for 1%

profile of v1, /device:TPU:4, one launch (start us, length us, event | category | flops | bytes accessed | tf_op | source)
XLA Modules:
  0.0 993.5 jit_solution(12629070498593775082)
XLA Ops:
  8.0 3.6 collective-permute-start.9
  11.6 129.3 %collective-permute-done.9 = bf16[1536,768]{1,0:T(8,128)(2,1)} collective-permute-done((bf16[1536,768]{1,0:T(8,128)(2,1)}, bf16[1536,768]{1,0:T(8,128)(2,1)}, u32[]{:S(2)}, u32[]{:S(2)}) %collective-permute-start.9) | collective-permute-done | bytes 2359328 | tf_op jit(solution)/shard_map/ppermute | solution.py:218
  147.2 36.8 %collective-permute-done.11 = bf16[1536,768]{1,0:T(8,128)(2,1)} collective-permute-done((bf16[1536,768]{1,0:T(8,128)(2,1)}, bf16[1536,768]{1,0:T(8,128)(2,1)}, u32[]{:S(2)}, u32[]{:S(2)}) %collective-permute-start.11) | collective-permute-done | bytes 2359328 | tf_op jit(solution)/shard_map/ppermute | solution.py:211
  184.0 4.9 broadcast_in_dim.14
  200.4 3.6 constant_dynamic-update-slice_fusion.6
  210.7 6.2 collective-permute-done
  217.0 4.9 broadcast_select_fusion.3
  221.8 18.2 %fusion.16 = bf16[1024,1536]{1,0:T(8,128)(2,1)} fusion(bf16[1536,3072]{1,0:T(8,128)(2,1)} %constant_dynamic-update-slice_fusion.4, bf16[512,3072]{1,0:T(8,128)(2,1)} %get-tuple-element.18, bf16[512,3072]{1,0:T(8,128)(2,1)} %get-tuple-element.17, bf16[1024,6144]{1,0:T(8,128)(2,1)} %param.13, s32[]{:T(128)S(6)} %select_n.85), kind=kOutput, calls=%fused_computation.25 | convolution fusion | flops 9693560832 | bytes 22020100 | tf_op jit(solution)/shard_map/td,gd->tg/dot_general | solution.py:290
  240.0 44.0 %collective-permute-done.18 = bf16[512,3072]{1,0:T(8,128)(2,1)} collective-permute-done((bf16[512,3072]{1,0:T(8,128)(2,1)}, bf16[512,3072]{1,0:T(8,128)(2,1)}, u32[]{:S(2)}, u32[]{:S(2)}) %collective-permute-start.18) | collective-permute-done | bytes 3145760 | tf_op jit(solution)/shard_map/ppermute | solution.py:211
  284.0 3.5 broadcast_select_fusion.1
  290.2 12.4 %convolution_convert_fusion = bf16[3072,1536]{1,0:T(8,128)(2,1)} fusion(bf16[1024,1536]{1,0:T(8,128)(2,1)S(1)} %copy-done.24, bf16[512,3072]{1,0:T(8,128)(2,1)S(1)} %get-tuple-element.16, bf16[512,3072]{1,0:T(8,128)(2,1)S(1)} %get-tuple-element.15), kind=kOutput, calls=%fused_computation.7 | convolution fusion | flops 9680977920 | bytes 18874368 | tf_op jit(solution)/shard_map/td,tq->dq/dot_general | solution.py:298
  304.8 23.6 %collective-permute-done.1 = bf16[384,768]{1,0:T(8,128)(2,1)} collective-permute-done((bf16[384,768]{1,0:T(8,128)(2,1)}, bf16[384,768]{1,0:T(8,128)(2,1)}, u32[]{:S(2)}, u32[]{:S(2)}) %collective-permute-start.1) | collective-permute-done | bytes 589856 | tf_op jit(solution)/shard_map/ppermute | solution.py:218
  328.5 27.7 %collective-permute-done.3 = bf16[384,768]{1,0:T(8,128)(2,1)} collective-permute-done((bf16[384,768]{1,0:T(8,128)(2,1)}, bf16[384,768]{1,0:T(8,128)(2,1)}, u32[]{:S(2)}, u32[]{:S(2)}) %collective-permute-start.3) | collective-permute-done | bytes 589856 | tf_op jit(solution)/shard_map/ppermute | solution.py:211
  365.4 14.1 %shard_map.128 = bf16[1024,1152]{1,0:T(8,128)(2,1)S(1)} custom-call(bf16[1024,1152]{1,0:T(8,128)(2,1)S(1)} %constant_dynamic-slice_fusion.keyed_ref, bf16[1024,384]{1,0:T(8,128)(2,1)S(1)} %fusion.23.grad_ref), custom_call_target="tpu_custom_call" | custom-call | flops 4026531840 | bytes 5505024 | tf_op jit(solution)/shard_map/pallas_call | solution.py:191
  380.9 10.3 %convolution_convert_fusion.1 = bf16[3072,1152]{1,0:T(8,128)(2,1)} fusion(bf16[1024,1152]{1,0:T(8,128)(2,1)S(1)} %shard_map.128, bf16[512,3072]{1,0:T(8,128)(2,1)S(1)} %copy-done.21, bf16[512,3072]{1,0:T(8,128)(2,1)S(1)} %copy-done.19), kind=kOutput, calls=%fused_computation.8 | convolution fusion | flops 7263879168 | bytes 15728640 | tf_op jit(solution)/shard_map/td,tq->dq/dot_general | solution.py:295
  393.2 5.0 collective-permute-start.5
  398.3 112.6 %collective-permute-done.13 = bf16[768,1536]{1,0:T(8,128)(2,1)} collective-permute-done((bf16[768,1536]{1,0:T(8,128)(2,1)}, bf16[768,1536]{1,0:T(8,128)(2,1)}, u32[]{:S(2)}, u32[]{:S(2)}) %collective-permute-start.13) | collective-permute-done | bytes 2359328 | tf_op jit(solution)/shard_map/ppermute | solution.py:218
  510.9 19.0 %collective-permute-done.5 = bf16[768,1152]{1,0:T(8,128)(2,1)} collective-permute-done((bf16[768,1152]{1,0:T(8,128)(2,1)}, bf16[768,1152]{1,0:T(8,128)(2,1)}, u32[]{:S(2)}, u32[]{:S(2)}) %collective-permute-start.5) | collective-permute-done | bytes 1769504 | tf_op jit(solution)/shard_map/ppermute | solution.py:218
  531.8 58.2 %collective-permute-done.15 = bf16[768,1536]{1,0:T(8,128)(2,1)} collective-permute-done((bf16[768,1536]{1,0:T(8,128)(2,1)}, bf16[768,1536]{1,0:T(8,128)(2,1)}, u32[]{:S(2)}, u32[]{:S(2)}) %collective-permute-start.15) | collective-permute-done | bytes 2359328 | tf_op jit(solution)/shard_map/ppermute | solution.py:211
  592.4 30.6 %collective-permute-done.7 = bf16[768,1152]{1,0:T(8,128)(2,1)} collective-permute-done((bf16[768,1152]{1,0:T(8,128)(2,1)}, bf16[768,1152]{1,0:T(8,128)(2,1)}, u32[]{:S(2)}, u32[]{:S(2)}) %collective-permute-start.7) | collective-permute-done | bytes 1769504 | tf_op jit(solution)/shard_map/ppermute | solution.py:211
  643.1 7.0 fusion.19
  650.1 9.9 add_convert_fusion.1
  661.6 3.9 fusion.18
  665.5 4.3 copy.16
  670.1 7.0 fusion.25
  677.1 10.7 %fusion.21 = f32[512,3072]{1,0:T(8,128)} fusion(bf16[3072,1536]{1,0:T(8,128)(2,1)} %copy-done.3, bf16[1024,1536]{1,0:T(8,128)(2,1)S(1)} %copy-done.26, s32[]{:T(128)S(6)} %select_n.84), kind=kOutput, calls=%fused_computation.39 | convolution fusion | flops 4831838208 | bytes 17301508 | tf_op jit(solution)/shard_map/tq,dq->td/dot_general | solution.py:309
  687.8 43.1 %collective-permute-done.17 = bf16[512,3072]{1,0:T(8,128)(2,1)} collective-permute-done((bf16[512,3072]{1,0:T(8,128)(2,1)}, bf16[512,3072]{1,0:T(8,128)(2,1)}, u32[]{:S(2)}, u32[]{:S(2)}) %collective-permute-start.17) | collective-permute-done | bytes 3145760 | tf_op jit(solution)/shard_map/ppermute | solution.py:211
  730.8 5.5 add_convert_fusion
  738.6 16.7 %fusion.6 = bf16[6144,768]{1,0:T(8,128)(2,1)} fusion(bf16[1024,6144]{1,0:T(8,128)(2,1)} %param.13, bf16[512,768]{1,0:T(8,128)(2,1)} %get-tuple-element.32, bf16[512,768]{1,0:T(8,128)(2,1)} %copy-done.22), kind=kOutput, calls=%fused_computation.13 | convolution fusion | flops 9709289472 | bytes 23592960 | tf_op jit(solution)/shard_map/tg,td->gd/dot_general | solution.py:275
  757.6 4.5 collective-permute-start.19
  762.1 166.3 %collective-permute-done.19 = bf16[768,1152]{1,0:T(8,128)(2,1)} collective-permute-done((bf16[768,1152]{1,0:T(8,128)(2,1)}, bf16[768,1152]{1,0:T(8,128)(2,1)}, u32[]{:S(2)}, u32[]{:S(2)}) %collective-permute-start.19) | collective-permute-done | bytes 1769504 | tf_op jit(solution)/shard_map/ppermute | solution.py:218
  928.4 51.8 %reduce-scatter.14.cloned.1.call-done = bf16[1536,768]{1,0:T(8,128)(2,1)} async-done(((bf16[6144,768]{1,0:T(8,128)(2,1)}), bf16[1536,768]{1,0:T(8,128)(2,1)}) %reduce-scatter.14.cloned.1.call-update) | async-done | bytes 2359312 | tf_op jit(solution)/shard_map/reduce_scatter | solution.py:279
  (132 shorter events, 79.6 us)
Async XLA Ops:
  7.2 654.4 %copy-start = (bf16[1024,1536]{1,0:T(8,128)(2,1)S(1)}, bf16[1024,1536]{1,0:T(8,128)(2,1)}, u32[]{:S(2)}) copy-start(bf16[1024,1536]{1,0:T(8,128)(2,1)} %param.12) | copy-start | bytes 9437188
  7.2 133.7 %all-gather.5.cloned.1.call-start = ((), (), s32[]{:S(2)}) async-start(), calls=%async_computation.9 | async-start | bytes 3932160 | tf_op jit(solution)/shard_map/all_gather | solution.py:244
  7.9 186.8 %all-gather.7.cloned.1.call-start = ((), (), s32[]{:S(2)}) async-start(), calls=%async_computation.10 | async-start | bytes 3932160 | tf_op jit(solution)/shard_map/all_gather | solution.py:244
  8.0 132.9 %collective-permute-start.9 = (bf16[1536,768]{1,0:T(8,128)(2,1)}, bf16[1536,768]{1,0:T(8,128)(2,1)}, u32[]{:S(2)}, u32[]{:S(2)}) collective-permute-start(bf16[1536,768]{1,0:T(8,128)(2,1)} %param.17), channel_id=1, source_target_pairs={{0,0},{1,8},{2,4},{3,12},{4,2},{5,10},{6,6},{7,14},{8,1},{9,9},{10... | collective-permute-start | bytes 7077896 | tf_op jit(solution)/shard_map/ppermute | solution.py:218
  11.6 743.7 %reduce-scatter.12.cloned.1.call-start = ((), (), s32[]{:S(2)}) async-start(), calls=%async_computation.7 | async-start | bytes 11796480 | tf_op jit(solution)/shard_map/reduce_scatter | solution.py:302
  140.9 43.1 %collective-permute-start.11 = (bf16[1536,768]{1,0:T(8,128)(2,1)}, bf16[1536,768]{1,0:T(8,128)(2,1)}, u32[]{:S(2)}, u32[]{:S(2)}) collective-permute-start(bf16[1536,768]{1,0:T(8,128)(2,1)} %collective-permute-done.9), channel_id=1, source_target_pairs={{0,8},{4,12},{8,0},{12,4},{1,9},{5,13},{9,1},{13,5},{2,10},{6,14},... | collective-permute-start | bytes 7077896 | tf_op jit(solution)/shard_map/ppermute | solution.py:211
  140.9 59.5 %collective-permute-start.10 = (bf16[1536,768]{1,0:T(8,128)(2,1)}, bf16[1536,768]{1,0:T(8,128)(2,1)}, u32[]{:S(2)}, u32[]{:S(2)}) collective-permute-start(bf16[1536,768]{1,0:T(8,128)(2,1)} %collective-permute-done.9), channel_id=1, source_target_pairs={{0,4},{4,0},{8,12},{12,8},{1,5},{5,1},{9,13},{13,9},{2,6},{6,2},{1... | collective-permute-start | bytes 7077896 | tf_op jit(solution)/shard_map/ppermute | solution.py:211
  145.8 71.2 %collective-permute-start = (bf16[512,3072]{1,0:T(8,128)(2,1)}, bf16[512,3072]{1,0:T(8,128)(2,1)}, u32[]{:S(2)}, u32[]{:S(2)}) collective-permute-start(bf16[512,3072]{1,0:T(8,128)(2,1)} %pad_maximum_fusion.6), channel_id=1, source_target_pairs={{0,16},{16,0},{1,17},{17,1},{2,18},{18,2},{3,19},{19,3},{4,20},{20... | collective-permute-start | bytes 9437192 | tf_op jit(solution)/shard_map/ppermute | solution.py:211
  184.0 23.3 %collective-permute-start.12 = (bf16[1536,768]{1,0:T(8,128)(2,1)}, bf16[1536,768]{1,0:T(8,128)(2,1)}, u32[]{:S(2)}, u32[]{:S(2)}) collective-permute-start(bf16[1536,768]{1,0:T(8,128)(2,1)} %collective-permute-done.11), channel_id=1, source_target_pairs={{0,4},{4,0},{8,12},{12,8},{1,5},{5,1},{9,13},{13,9},{2,6},{6,2},{1... | collective-permute-start | bytes 7077896 | tf_op jit(solution)/shard_map/ppermute | solution.py:211
  198.8 85.1 %collective-permute-start.18 = (bf16[512,3072]{1,0:T(8,128)(2,1)}, bf16[512,3072]{1,0:T(8,128)(2,1)}, u32[]{:S(2)}, u32[]{:S(2)}) collective-permute-start(bf16[512,3072]{1,0:T(8,128)(2,1)} %pad_maximum_fusion.8), channel_id=1, source_target_pairs={{0,16},{16,0},{1,17},{17,1},{2,18},{18,2},{3,19},{19,3},{4,20},{20... | collective-permute-start | bytes 9437192 | tf_op jit(solution)/shard_map/ppermute | solution.py:211
  240.0 50.2 %copy-start.24 = (bf16[1024,1536]{1,0:T(8,128)(2,1)S(1)}, bf16[1024,1536]{1,0:T(8,128)(2,1)}, u32[]{:S(2)}) copy-start(bf16[1024,1536]{1,0:T(8,128)(2,1)} %fusion.16) | copy-start | bytes 9437188
  302.7 454.9 %reduce-scatter.10.cloned.1.call-start = ((), (), s32[]{:S(2)}) async-start(), calls=%async_computation.6 | async-start | bytes 8847360 | tf_op jit(solution)/shard_map/reduce_scatter | solution.py:301
  302.7 25.7 %collective-permute-start.1 = (bf16[384,768]{1,0:T(8,128)(2,1)}, bf16[384,768]{1,0:T(8,128)(2,1)}, u32[]{:S(2)}, u32[]{:S(2)}) collective-permute-start(bf16[384,768]{1,0:T(8,128)(2,1)} %param.16), channel_id=1, source_target_pairs={{0,0},{1,8},{2,4},{3,12},{4,2},{5,10},{6,6},{7,14},{8,1},{9,9},{10... | collective-permute-start | bytes 1769480 | tf_op jit(solution)/shard_map/ppermute | solution.py:218
  328.4 27.7 %collective-permute-start.3 = (bf16[384,768]{1,0:T(8,128)(2,1)}, bf16[384,768]{1,0:T(8,128)(2,1)}, u32[]{:S(2)}, u32[]{:S(2)}) collective-permute-start(bf16[384,768]{1,0:T(8,128)(2,1)} %collective-permute-done.1), channel_id=1, source_target_pairs={{0,8},{4,12},{8,0},{12,4},{1,9},{5,13},{9,1},{13,5},{2,10},{6,14},... | collective-permute-start | bytes 1769480 | tf_op jit(solution)/shard_map/ppermute | solution.py:211
  328.4 31.0 %collective-permute-start.2 = (bf16[384,768]{1,0:T(8,128)(2,1)}, bf16[384,768]{1,0:T(8,128)(2,1)}, u32[]{:S(2)}, u32[]{:S(2)}) collective-permute-start(bf16[384,768]{1,0:T(8,128)(2,1)} %collective-permute-done.1), channel_id=1, source_target_pairs={{0,4},{4,0},{8,12},{12,8},{1,5},{5,1},{9,13},{13,9},{2,6},{6,2},{1... | collective-permute-start | bytes 1769480 | tf_op jit(solution)/shard_map/ppermute | solution.py:211
  356.2 5.6 collective-permute-start.4
  391.2 537.1 %reduce-scatter.16.cloned.1.call-start = ((), (), s32[]{:S(2)}) async-start(), calls=%async_computation.11 | async-start | bytes 2949120
  391.3 119.6 %collective-permute-start.13 = (bf16[768,1536]{1,0:T(8,128)(2,1)}, bf16[768,1536]{1,0:T(8,128)(2,1)}, u32[]{:S(2)}, u32[]{:S(2)}) collective-permute-start(bf16[768,1536]{1,0:T(8,128)(2,1)} %param.15), channel_id=1, source_target_pairs={{0,0},{1,8},{2,4},{3,12},{4,2},{5,10},{6,6},{7,14},{8,1},{9,9},{10... | collective-permute-start | bytes 7077896 | tf_op jit(solution)/shard_map/ppermute | solution.py:218
  393.2 136.7 %collective-permute-start.5 = (bf16[768,1152]{1,0:T(8,128)(2,1)}, bf16[768,1152]{1,0:T(8,128)(2,1)}, u32[]{:S(2)}, u32[]{:S(2)}) collective-permute-start(bf16[768,1152]{1,0:T(8,128)(2,1)} %param.14), channel_id=1, source_target_pairs={{0,0},{1,8},{2,4},{3,12},{4,2},{5,10},{6,6},{7,14},{8,1},{9,9},{10... | collective-permute-start | bytes 5308424 | tf_op jit(solution)/shard_map/ppermute | solution.py:218
  510.9 79.1 %collective-permute-start.15 = (bf16[768,1536]{1,0:T(8,128)(2,1)}, bf16[768,1536]{1,0:T(8,128)(2,1)}, u32[]{:S(2)}, u32[]{:S(2)}) collective-permute-start(bf16[768,1536]{1,0:T(8,128)(2,1)} %collective-permute-done.13), channel_id=1, source_target_pairs={{0,8},{4,12},{8,0},{12,4},{1,9},{5,13},{9,1},{13,5},{2,10},{6,14},... | collective-permute-start | bytes 7077896 | tf_op jit(solution)/shard_map/ppermute | solution.py:211
  529.9 93.1 %collective-permute-start.7 = (bf16[768,1152]{1,0:T(8,128)(2,1)}, bf16[768,1152]{1,0:T(8,128)(2,1)}, u32[]{:S(2)}, u32[]{:S(2)}) collective-permute-start(bf16[768,1152]{1,0:T(8,128)(2,1)} %collective-permute-done.5), channel_id=1, source_target_pairs={{0,8},{4,12},{8,0},{12,4},{1,9},{5,13},{9,1},{13,5},{2,10},{6,14},... | collective-permute-start | bytes 5308424 | tf_op jit(solution)/shard_map/ppermute | solution.py:211
  529.9 101.8 %collective-permute-start.6 = (bf16[768,1152]{1,0:T(8,128)(2,1)}, bf16[768,1152]{1,0:T(8,128)(2,1)}, u32[]{:S(2)}, u32[]{:S(2)}) collective-permute-start(bf16[768,1152]{1,0:T(8,128)(2,1)} %collective-permute-done.5), channel_id=1, source_target_pairs={{0,4},{4,0},{8,12},{12,8},{1,5},{5,1},{9,13},{13,9},{2,6},{6,2},{1... | collective-permute-start | bytes 5308424 | tf_op jit(solution)/shard_map/ppermute | solution.py:211
  529.9 107.5 %collective-permute-start.14 = (bf16[768,1536]{1,0:T(8,128)(2,1)}, bf16[768,1536]{1,0:T(8,128)(2,1)}, u32[]{:S(2)}, u32[]{:S(2)}) collective-permute-start(bf16[768,1536]{1,0:T(8,128)(2,1)} %collective-permute-done.13), channel_id=1, source_target_pairs={{0,4},{4,0},{8,12},{12,8},{1,5},{5,1},{9,13},{13,9},{2,6},{6,2},{1... | collective-permute-start | bytes 7077896 | tf_op jit(solution)/shard_map/ppermute | solution.py:211
  530.4 59.6 %collective-permute-start.21 = (bf16[512,768]{1,0:T(8,128)(2,1)}, bf16[512,768]{1,0:T(8,128)(2,1)}, u32[]{:S(2)}, u32[]{:S(2)}) collective-permute-start(bf16[512,768]{1,0:T(8,128)(2,1)} %param.10), channel_id=1, source_target_pairs={{0,16},{16,0},{1,17},{17,1},{2,18},{18,2},{3,19},{19,3},{4,20},{20... | collective-permute-start | bytes 2359304 | tf_op jit(solution)/shard_map/ppermute | solution.py:211
  590.0 52.8 %collective-permute-start.16 = (bf16[768,1536]{1,0:T(8,128)(2,1)}, bf16[768,1536]{1,0:T(8,128)(2,1)S(1)}, u32[]{:S(2)}, u32[]{:S(2)}) collective-permute-start(bf16[768,1536]{1,0:T(8,128)(2,1)} %collective-permute-done.15), channel_id=1, source_target_pairs={{0,4},{4,0},{8,12},{12,8},{1,5},{5,1},{9,13},{13,9},{2,6},{6,2},{1... | collective-permute-start | bytes 7077896 | tf_op jit(solution)/shard_map/ppermute | solution.py:211
  592.4 69.2 %copy-start.22 = (bf16[512,768]{1,0:T(8,128)(2,1)}, bf16[512,768]{1,0:T(8,128)(2,1)S(1)}, u32[]{:S(2)}) copy-start(bf16[512,768]{1,0:T(8,128)(2,1)S(1)} %get-tuple-element.31) | copy-start | bytes 2359300
  623.0 18.4 %collective-permute-start.8 = (bf16[768,1152]{1,0:T(8,128)(2,1)}, bf16[768,1152]{1,0:T(8,128)(2,1)S(1)}, u32[]{:S(2)}, u32[]{:S(2)}) collective-permute-start(bf16[768,1152]{1,0:T(8,128)(2,1)} %collective-permute-done.7), channel_id=1, source_target_pairs={{0,4},{4,0},{8,12},{12,8},{1,5},{5,1},{9,13},{13,9},{2,6},{6,2},{1... | collective-permute-start | bytes 5308424 | tf_op jit(solution)/shard_map/ppermute | solution.py:211
  660.0 70.8 %collective-permute-start.17 = (bf16[512,3072]{1,0:T(8,128)(2,1)}, bf16[512,3072]{1,0:T(8,128)(2,1)}, u32[]{:S(2)}, u32[]{:S(2)}) collective-permute-start(bf16[512,3072]{1,0:T(8,128)(2,1)} %add_convert_fusion.1), channel_id=1, source_target_pairs={{0,16},{16,0},{1,17},{17,1},{2,18},{18,2},{3,19},{19,3},{4,20},{20... | collective-permute-start | bytes 9437192 | tf_op jit(solution)/shard_map/ppermute | solution.py:211
  669.8 258.6 %reduce-scatter.8.cloned.1.call-start = ((), (), s32[]{:S(2)}) async-start(), calls=%async_computation.5 | async-start | bytes 3932160 | tf_op jit(solution)/shard_map/reduce_scatter | solution.py:317
  738.5 241.7 %reduce-scatter.14.cloned.1.call-start = ((), (), s32[]{:S(2)}) async-start(), calls=%async_computation.8 | async-start | bytes 11796480 | tf_op jit(solution)/shard_map/reduce_scatter | solution.py:279
  755.3 173.1 %collective-permute-start.20 = (bf16[768,1536]{1,0:T(8,128)(2,1)}, bf16[768,1536]{1,0:T(8,128)(2,1)}, u32[]{:S(2)}, u32[]{:S(2)}) collective-permute-start(bf16[768,1536]{1,0:T(8,128)(2,1)} %reduce-scatter.12.cloned.1.call-done), channel_id=1, source_target_pairs={{0,0},{1,8},{2,4},{3,12},{4,2},{5,10},{6,6},{7,14},{8,1},{9,9},{10... | collective-permute-start | bytes 7077896 | tf_op jit(solution)/shard_map/ppermute | solution.py:218
  757.6 170.8 %collective-permute-start.19 = (bf16[768,1152]{1,0:T(8,128)(2,1)}, bf16[768,1152]{1,0:T(8,128)(2,1)}, u32[]{:S(2)}, u32[]{:S(2)}) collective-permute-start(bf16[768,1152]{1,0:T(8,128)(2,1)} %reduce-scatter.10.cloned.1.call-done), channel_id=1, source_target_pairs={{0,0},{1,8},{2,4},{3,12},{4,2},{5,10},{6,6},{7,14},{8,1},{9,9},{10... | collective-permute-start | bytes 5308424 | tf_op jit(solution)/shard_map/ppermute | solution.py:218
  (24 other events, 303.9 us)
Sparse Core Ops, SparseCore 0:
  9.6 104.7 all-gather.4
  115.9 78.6 all-gather.6
  302.8 90.0 reduce-scatter.11
  395.3 155.3 reduce-scatter.9
  669.9 29.3 reduce-scatter.15
  738.6 91.2 reduce-scatter.7
  833.0 147.0 reduce-scatter.13

commit v2 on v1

--- a/solution.py
+++ b/solution.py
@@ -218,31 +218,20 @@
     return lax.ppermute(block, ("gy", "gz"), pairs)
 
 
-def gather_width(block, dim):
-    place = lax.axis_index("gy")
-    width = block.shape[dim]
-    shape = list(block.shape)
-    shape[dim] = 4 * width
-    whole = jnp.zeros(tuple(shape), block.dtype)
+def after(value, *earlier):
+    return lax.optimization_barrier((value,) + earlier)[0]
+
+
+def four_parts(block):
+    opposite = exchange(block, "gy", 2)
     beside = exchange(block, "gy", 1)
-    opposite = exchange(block, "gy", 2)
-    last = exchange(opposite, "gy", 1)
-    for flip, part in ((0, block), (1, beside), (2, opposite), (3, last)):
-        whole = lax.dynamic_update_slice_in_dim(
-            whole, part, lax.bitwise_xor(place, flip) * width, dim
-        )
-    return whole
+    return block, beside, opposite, exchange(opposite, "gy", 1)
 
 
 def both_halves(half):
     other = exchange(half, "gx", 1)
     first = lax.axis_index("gx") == 0
     return jnp.concatenate([jnp.where(first, half, other), jnp.where(first, other, half)], axis=0)
-
-
-def whole_width(rows):
-    blocks = lax.all_gather(rows, "gz", axis=0)
-    return jnp.concatenate([blocks[SWAP[i]] for i in range(4)], axis=1)
 
 
 def local_columns(
@@ -257,17 +246,16 @@
     hidden_out,
 ):
     side = lax.axis_index("gx")
+    place = lax.axis_index("gy")
     deep = lax.axis_index("gz")
     column = 2 * lax.rem(deep, 2) + deep // 2
-    half = normed.shape[0]
+    half, block = normed.shape
+    width = attend_in.shape[1]
+    units = hidden_in.shape[1]
+
+    grad_blocks = lax.all_gather(out_grad, "gz", axis=0)
+    turned_out = turn(jnp.concatenate([hidden_out, attend_out], axis=0))
     grad_own = both_halves(out_grad)
-    grad_slab = both_halves(whole_width(out_grad))
-    attend_rows = gather_width(turn(attend_out), 1)
-    hidden_rows = gather_width(turn(hidden_out), 1)
-    normed_slab = both_halves(whole_width(normed))
-    attend_cols = gather_width(turn(attend_in), 0)
-    hidden_cols = gather_width(turn(hidden_in), 0)
-
     activated = gelu_value(hidden_pre.astype(jnp.float32)).astype(jnp.bfloat16)
     part_attend_out = jnp.einsum(
         "tg,td->gd", mixed_heads, grad_own, preferred_element_type=jnp.float32
@@ -275,31 +263,63 @@
     part_hidden_out = jnp.einsum(
         "tg,td->gd", activated, grad_own, preferred_element_type=jnp.float32
     ).astype(jnp.bfloat16)
-    attend_out_grad = lax.psum_scatter(part_attend_out, "gy", scatter_dimension=0, tiled=True)
-    hidden_out_grad = lax.psum_scatter(part_hidden_out, "gy", scatter_dimension=0, tiled=True)
-
-    head_grad = jnp.einsum(
-        "td,gd->tg", grad_slab, attend_rows, preferred_element_type=jnp.float32
-    ).astype(jnp.bfloat16)
-    width = attend_in.shape[1]
-    keyed = lax.dynamic_slice_in_dim(projected, column * width, width, 1)
-    projected_grad = attention_backward(keyed, head_grad)
-
-    units = hidden_in.shape[1]
+
+    normed_blocks = lax.all_gather(
+        after(normed, grad_blocks, part_attend_out, part_hidden_out), "gz", axis=0
+    )
+    out_parts = four_parts(turned_out)
+    in_block = jnp.concatenate([hidden_in, attend_in], axis=1)
+    turned_in = turn(after(in_block, out_parts[2]))
+    hidden_out_grad = lax.psum_scatter(
+        after(part_hidden_out, normed_blocks), "gy", scatter_dimension=0, tiled=True
+    )
+    attend_out_grad = lax.psum_scatter(
+        after(part_attend_out, hidden_out_grad), "gy", scatter_dimension=0, tiled=True
+    )
+
+    order = []
+    for flip in range(4):
+        slot = lax.bitwise_xor(place, flip)
+        order.append(2 * lax.rem(slot, 2) + slot // 2)
+    grad_slab = both_halves(
+        jnp.concatenate(
+            [lax.dynamic_index_in_dim(grad_blocks, at, 0, keepdims=False) for at in order], axis=1
+        )
+    )
+    normed_slab = both_halves(jnp.concatenate([normed_blocks[at] for at in SWAP], axis=1))
+    hidden_rows = jnp.concatenate([part[:units] for part in out_parts], axis=1)
+    attend_rows = jnp.concatenate([part[units:] for part in out_parts], axis=1)
+
     pre_here = lax.dynamic_slice_in_dim(hidden_pre, column * units, units, 1)
     hidden_part = jnp.einsum(
         "td,gd->tg", grad_slab, hidden_rows, preferred_element_type=jnp.float32
     )
     hidden_grad = (hidden_part * gelu_slope(pre_here.astype(jnp.float32))).astype(jnp.bfloat16)
-
+    part_hidden_in = jnp.einsum(
+        "td,tq->dq", normed_slab, hidden_grad, preferred_element_type=jnp.float32
+    ).astype(jnp.bfloat16)
+
+    head_grad = jnp.einsum(
+        "td,gd->tg", grad_slab, attend_rows, preferred_element_type=jnp.float32
+    ).astype(jnp.bfloat16)
+    keyed = lax.dynamic_slice_in_dim(projected, column * width, width, 1)
+    projected_grad = attention_backward(keyed, head_grad)
     part_attend_in = jnp.einsum(
         "td,tq->dq", normed_slab, projected_grad, preferred_element_type=jnp.float32
     ).astype(jnp.bfloat16)
-    part_hidden_in = jnp.einsum(
-        "td,tq->dq", normed_slab, hidden_grad, preferred_element_type=jnp.float32
-    ).astype(jnp.bfloat16)
-    attend_in_grad = turn(lax.psum_scatter(part_attend_in, "gy", scatter_dimension=0, tiled=True))
-    hidden_in_grad = turn(lax.psum_scatter(part_hidden_in, "gy", scatter_dimension=0, tiled=True))
+
+    hidden_in_sum = lax.psum_scatter(
+        after(part_hidden_in, attend_out_grad, turned_in), "gy", scatter_dimension=0, tiled=True
+    )
+    attend_in_sum = lax.psum_scatter(
+        after(part_attend_in, hidden_in_sum), "gy", scatter_dimension=0, tiled=True
+    )
+    hidden_in_grad = turn(hidden_in_sum)
+    attend_in_grad = turn(attend_in_sum)
+
+    in_parts = four_parts(turned_in)
+    hidden_cols = jnp.concatenate([part[:, :units] for part in in_parts], axis=0)
+    attend_cols = jnp.concatenate([part[:, units:] for part in in_parts], axis=0)
 
     def input_grad(start):
         attend_part = lax.dynamic_slice_in_dim(projected_grad, start, half, 0)
@@ -310,11 +330,18 @@
 
     arrived = exchange(input_grad((1 - side) * half).astype(jnp.bfloat16), "gx", 1)
     row_grad = (input_grad(side * half) + arrived.astype(jnp.float32)).astype(jnp.bfloat16)
-    block = normed.shape[1]
     row_grad = jnp.concatenate(
-        [row_grad[:, SWAP[i] * block : (SWAP[i] + 1) * block] for i in range(4)], axis=1
-    )
-    normed_grad = lax.psum_scatter(row_grad, "gz", scatter_dimension=1, tiled=True)
+        [
+            lax.dynamic_slice_in_dim(
+                row_grad, lax.bitwise_xor(place, SWAP[at]) * block, block, 1
+            )
+            for at in range(4)
+        ],
+        axis=1,
+    )
+    normed_grad = lax.psum_scatter(
+        after(row_grad, attend_in_sum), "gz", scatter_dimension=1, tiled=True
+    )
     return normed_grad, attend_in_grad, hidden_in_grad, attend_out_grad, hidden_out_grad
 
 

time: 1010 us -> 933 us (0.924)
  waiting for transfers between devices: 753 us -> 668 us
  matrix products: 99.4 us -> 112 us
    ppermute x6 -> x4, waiting for transfers between devices: 451 us -> 286 us  [turn(): return lax.ppermute(block, ('gy', 'gz'), pairs)]
    all_gather x2, waiting for transfers between devices: 2.5 us -> 82.9 us  [the longest x1 68.7 us: local_columns(): grad_blocks = lax.all_gather(out_grad, 'gz', axis=0)]
    slice x3 -> x17, local copies, waits for them, and re-layouts: 4.3 us -> 44.4 us  [the longest x4 13 us: local_columns(): hidden_rows = jnp.concatenate([part[:units] for part in out_parts], axis=1)]
    dynamic_update_slice x16 -> x0, local copies, waits for them, and re-layouts: 33.3 us -> none  [gather_width(): lax.dynamic_update_slice_in_dim(whole, part, lax.bitwise_xor(place, flip)...]
    reduce_scatter x4, waiting for transfers between devices: 51.9 us -> 38 us  [the longest x1 38 us: local_columns(): lax.psum_scatter(after(part_hidden_in, attend_out_grad, turned_in), 'gy',...]
    ppermute x16 -> x10, waiting for transfers between devices: 247 us -> 260 us  [exchange(): return lax.ppermute(block, axis, [(i, i ^ flip) for i in range(size)])]
  transfers between devices with their start and end apart: 29 -> 21, of which waited for: 14 -> 13; matrix products, arithmetic and copies ran while one was open for 16% -> 21% of each run, Pallas kernels for 1% -> 2%
where the time goes in v2:
time: 933 us; the launch traced here: 921 us
  waiting for transfers between devices  668 us (72%)
  matrix products  112 us (12%)
  local copies, waits for them, and re-layouts  61.2 us (7%)
  other arithmetic  29.6 us (3%)
  starting transfers between devices  20.5 us (2%)
  between operations  14.9 us (2%)
  Pallas kernels  14.1 us (2%)
    ppermute x4, waiting for transfers between devices, turn(): return lax.ppermute(block, ('gy', 'gz'), pairs)  286 us
    ppermute x10, waiting for transfers between devices, exchange(): return lax.ppermute(block, axis, [(i, i ^ flip) for i in range(size)])  260 us
    all_gather x1, waiting for transfers between devices, local_columns(): grad_blocks = lax.all_gather(out_grad, 'gz', axis=0)  68.7 us
    reduce_scatter x1, waiting for transfers between devices, local_columns(): lax.psum_scatter(after(part_hidden_in, attend_out_grad, turned_in), 'gy',...  38 us
    dot_general x2, matrix products, input_grad(): jnp.einsum('tq,dq->td', hidden_part, hidden_cols, preferred_element_type=...  25.5 us
    dot_general x2, matrix products, input_grad(): jnp.einsum('tq,dq->td', attend_part, attend_cols, preferred_element_type=...  19.2 us
  transfers between devices with their start and end apart: 21, of which 13 were waited for; matrix products, arithmetic and copies ran while one was open for 21% of the time, Pallas kernels for 2%

profile of v2, /device:TPU:4, one launch (start us, length us, event | category | flops | bytes accessed | tf_op | source)
XLA Modules:
  0.0 920.7 jit_solution(17314160521823230582)
XLA Ops:
  9.5 3.7 pad_maximum_fusion.12
  13.2 3.4 collective-permute-start.1
  16.7 11.0 %collective-permute-done.10 = bf16[512,768]{1,0:T(8,128)(2,1)} collective-permute-done((bf16[512,768]{1,0:T(8,128)(2,1)}, bf16[512,768]{1,0:T(8,128)(2,1)}, u32[]{:S(2)}, u32[]{:S(2)}) %collective-permute-start.10) | collective-permute-done | bytes 786464 | tf_op jit(solution)/shard_map/ppermute | solution.py:211
  30.2 16.5 %fusion.6 = bf16[6144,768]{1,0:T(8,128)(2,1)} fusion(bf16[1024,6144]{1,0:T(8,128)(2,1)} %param.13, bf16[512,768]{1,0:T(8,128)(2,1)S(1)} %get-tuple-element.46, bf16[512,768]{1,0:T(8,128)(2,1)S(1)} %get-tuple-element.45), kind=kOutput, calls=%fused_computation.13 | convolution fusion | flops 9709289472 | bytes 23592960 | tf_op jit(solution)/shard_map/tg,td->gd/dot_general | solution.py:263
  46.7 5.4 fusion.28
  52.1 68.7 %all-gather.5.cloned.1.call-done = bf16[2048,768]{1,0:T(8,128)(2,1)} async-done(((bf16[512,768]{1,0:T(8,128)(2,1)}), bf16[2048,768]{1,0:T(8,128)(2,1)}) %all-gather.5.cloned.1.call-update) | async-done | bytes 3145744 | tf_op jit(solution)/shard_map/all_gather | solution.py:256
  120.9 71.4 %collective-permute-done.1 = bf16[1920,768]{1,0:T(8,128)(2,1)} collective-permute-done((bf16[1920,768]{1,0:T(8,128)(2,1)}, bf16[1920,768]{1,0:T(8,128)(2,1)}, u32[]{:S(2)}, u32[]{:S(2)}) %collective-permute-start.1) | collective-permute-done | bytes 2949152 | tf_op jit(solution)/shard_map/ppermute | solution.py:218
  197.3 14.2 %all-gather.7.cloned.1.call-done = bf16[2048,768]{1,0:T(8,128)(2,1)} async-done(((bf16[512,768]{1,0:T(8,128)(2,1)}), bf16[2048,768]{1,0:T(8,128)(2,1)}) %all-gather.7.cloned.1.call-update) | async-done | bytes 3145744 | tf_op jit(solution)/shard_map/all_gather | solution.py:267
  217.0 11.0 %collective-permute-done.3 = bf16[1920,768]{1,0:T(8,128)(2,1)} collective-permute-done((bf16[1920,768]{1,0:T(8,128)(2,1)}, bf16[1920,768]{1,0:T(8,128)(2,1)}, u32[]{:S(2)}, u32[]{:S(2)}) %collective-permute-start.3) | collective-permute-done | bytes 2949152 | tf_op jit(solution)/shard_map/ppermute | solution.py:211
  228.1 4.5 pad_maximum_fusion.4
  251.4 50.9 %collective-permute-done.11 = bf16[512,3072]{1,0:T(8,128)(2,1)} collective-permute-done((bf16[512,3072]{1,0:T(8,128)(2,1)}, bf16[512,3072]{1,0:T(8,128)(2,1)}, u32[]{:S(2)}, u32[]{:S(2)}) %collective-permute-start.11) | collective-permute-done | bytes 3145760 | tf_op jit(solution)/shard_map/ppermute | solution.py:211
  302.3 8.5 broadcast_select_fusion.1
  310.8 17.5 %fusion.24 = bf16[1024,1536]{1,0:T(8,128)(2,1)} fusion(bf16[1536,768]{1,0:T(8,128)(2,1)} %slice.95, bf16[1536,768]{1,0:T(8,128)(2,1)} %slice.94, bf16[1536,768]{1,0:T(8,128)(2,1)} %slice.93, bf16[1536,768]{1,0:T(8,128)(2,1)} %slice.92, bf16[512,3072]{1,0:T(8,128)(2,1)} %get-tuple-element.47, bf16[512,3072]{1,0:T(8,128)(2,1)} %get-tuple-element.48, ...), kind=kOutput, calls=%fused_computation.35 | convolution fusion | flops 9731309568 | bytes 22020100 | tf_op jit(solution)/shard_map/td,gd->tg/dot_general | solution.py:294
  328.3 14.7 %convolution_convert_fusion = bf16[3072,1536]{1,0:T(8,128)(2,1)} fusion(bf16[1024,1536]{1,0:T(8,128)(2,1)} %fusion.24, bf16[512,3072]{1,0:T(8,128)(2,1)} %get-tuple-element.30, bf16[512,3072]{1,0:T(8,128)(2,1)S(1)} %copy-done.10), kind=kOutput, calls=%fused_computation.7 | convolution fusion | flops 9680977920 | bytes 18874368 | tf_op jit(solution)/shard_map/td,tq->dq/dot_general | solution.py:298
  343.0 31.4 %collective-permute-done.5 = bf16[768,2688]{1,0:T(8,128)(2,1)} collective-permute-done((bf16[768,2688]{1,0:T(8,128)(2,1)}, bf16[768,2688]{1,0:T(8,128)(2,1)}, u32[]{:S(2)}, u32[]{:S(2)}) %collective-permute-start.5) | collective-permute-done | bytes 4128800 | tf_op jit(solution)/shard_map/ppermute | solution.py:218
  383.3 3.4 fusion.40.grad_ref
  386.7 14.1 %shard_map.128 = bf16[1024,1152]{1,0:T(8,128)(2,1)S(1)} custom-call(bf16[1024,1152]{1,0:T(8,128)(2,1)S(1)} %constant_dynamic-slice_fusion.4.keyed_ref, bf16[1024,384]{1,0:T(8,128)(2,1)S(1)} %fusion.40.grad_ref), custom_call_target="tpu_custom_call" | custom-call | flops 4026531840 | bytes 5505024 | tf_op jit(solution)/shard_map/pallas_call | solution.py:191
  400.9 10.2 %convolution_convert_fusion.1 = bf16[3072,1152]{1,0:T(8,128)(2,1)} fusion(bf16[1024,1152]{1,0:T(8,128)(2,1)S(1)} %shard_map.128, bf16[512,3072]{1,0:T(8,128)(2,1)S(1)} %copy-done.12, bf16[512,3072]{1,0:T(8,128)(2,1)S(1)} %copy-done.11), kind=kOutput, calls=%fused_computation.8 | convolution fusion | flops 7263879168 | bytes 15728640 | tf_op jit(solution)/shard_map/td,tq->dq/dot_general | solution.py:307
  411.1 38.0 %reduce-scatter.10.cloned.1.call-done = bf16[768,1536]{1,0:T(8,128)(2,1)} async-done(((bf16[3072,1536]{1,0:T(8,128)(2,1)}), bf16[768,1536]{1,0:T(8,128)(2,1)}) %reduce-scatter.10.cloned.1.call-update) | async-done | bytes 2359312 | tf_op jit(solution)/shard_map/reduce_scatter | solution.py:311
  451.1 140.2 %collective-permute-done.7 = bf16[768,2688]{1,0:T(8,128)(2,1)} collective-permute-done((bf16[768,2688]{1,0:T(8,128)(2,1)}, bf16[768,2688]{1,0:T(8,128)(2,1)}, u32[]{:S(2)}, u32[]{:S(2)}) %collective-permute-start.7) | collective-permute-done | bytes 4128800 | tf_op jit(solution)/shard_map/ppermute | solution.py:211
  598.6 3.7 slice.90
  602.3 3.4 slice.97
  614.9 12.8 %fusion.36 = f32[512,3072]{1,0:T(8,128)} fusion(bf16[768,1536]{1,0:T(8,128)(2,1)} %slice.99, bf16[768,1536]{1,0:T(8,128)(2,1)S(1)} %slice.98, bf16[768,1536]{1,0:T(8,128)(2,1)} %slice.97, bf16[768,1536]{1,0:T(8,128)(2,1)S(1)} %slice.96, bf16[1024,1536]{1,0:T(8,128)(2,1)} %fusion.24, s32[]{:T(128)S(6)} %select_n.103), kind=kOutput, calls=%fused_computation.55 | convolution fusion | flops 4869586944 | bytes 17301508 | tf_op jit(solution)/shard_map/tq,dq->td/dot_general | solution.py:329
  627.6 10.6 %add_convert_fusion.1 = bf16[512,3072]{1,0:T(8,128)(2,1)} fusion(f32[512,3072]{1,0:T(8,128)} %fusion.36, bf16[768,1152]{1,0:T(8,128)(2,1)} %slice.91, bf16[768,1152]{1,0:T(8,128)(2,1)} %slice.90, bf16[768,1152]{1,0:T(8,128)(2,1)} %slice.89, bf16[768,1152]{1,0:T(8,128)(2,1)S(1)} %slice.88, bf16[1024,1152]{1,0:T(8,128)(2,1)S(1)} %shard_map.128, s32[]{:T(128)S(6)} %select_n.103), kind=kOutput, calls=%fused_computation.34 | convolution fusion | flops 3655335936 | bytes 17694724 | tf_op jit(solution)/shard_map/tq,dq->td/dot_general | solution.py:327
  639.7 4.3 copy.16
  644.4 8.6 fusion.43
  653.0 12.7 %fusion.37 = f32[512,3072]{1,0:T(8,128)} fusion(bf16[768,1536]{1,0:T(8,128)(2,1)} %slice.99, bf16[768,1536]{1,0:T(8,128)(2,1)} %copy-done.16, bf16[768,1536]{1,0:T(8,128)(2,1)} %slice.97, bf16[768,1536]{1,0:T(8,128)(2,1)} %copy-done.15, bf16[1024,1536]{1,0:T(8,128)(2,1)} %fusion.24, s32[]{:T(128)S(6)} %select_n.101), kind=kOutput, calls=%fused_computation.56 | convolution fusion | flops 4869586944 | bytes 17301508 | tf_op jit(solution)/shard_map/tq,dq->td/dot_general | solution.py:329
  665.7 43.2 %collective-permute-done.9 = bf16[512,3072]{1,0:T(8,128)(2,1)} collective-permute-done((bf16[512,3072]{1,0:T(8,128)(2,1)}, bf16[512,3072]{1,0:T(8,128)(2,1)}, u32[]{:S(2)}, u32[]{:S(2)}) %collective-permute-start.9) | collective-permute-done | bytes 3145760 | tf_op jit(solution)/shard_map/ppermute | solution.py:211
  708.9 5.6 add_convert_fusion
  716.7 5.5 collective-permute-start.13
  724.2 164.2 %collective-permute-done.13 = bf16[768,1536]{1,0:T(8,128)(2,1)} collective-permute-done((bf16[768,1536]{1,0:T(8,128)(2,1)}, bf16[768,1536]{1,0:T(8,128)(2,1)}, u32[]{:S(2)}, u32[]{:S(2)}) %collective-permute-start.13) | collective-permute-done | bytes 2359328 | tf_op jit(solution)/shard_map/ppermute | solution.py:218
  888.4 19.0 %collective-permute-done.12 = bf16[768,1152]{1,0:T(8,128)(2,1)} collective-permute-done((bf16[768,1152]{1,0:T(8,128)(2,1)}, bf16[768,1152]{1,0:T(8,128)(2,1)}, u32[]{:S(2)}, u32[]{:S(2)}) %collective-permute-start.12) | collective-permute-done | bytes 1769504 | tf_op jit(solution)/shard_map/ppermute | solution.py:218
  (99 shorter events, 73.4 us)
Async XLA Ops:
  7.2 39.6 %copy-start = (bf16[1024,1536]{1,0:T(8,128)(2,1)S(1)}, bf16[1024,1536]{1,0:T(8,128)(2,1)}, u32[]{:S(2)}) copy-start(bf16[1024,1536]{1,0:T(8,128)(2,1)} %param.12) | copy-start | bytes 9437188
  7.2 113.6 %all-gather.5.cloned.1.call-start = ((), (), s32[]{:S(2)}) async-start(), calls=%async_computation.9 | async-start | bytes 3932160 | tf_op jit(solution)/shard_map/all_gather | solution.py:256
  7.9 203.6 %all-gather.7.cloned.1.call-start = ((), (), s32[]{:S(2)}) async-start(), calls=%async_computation.10 | async-start | bytes 3932160 | tf_op jit(solution)/shard_map/all_gather | solution.py:267
  8.0 19.7 %collective-permute-start.10 = (bf16[512,768]{1,0:T(8,128)(2,1)}, bf16[512,768]{1,0:T(8,128)(2,1)}, u32[]{:S(2)}, u32[]{:S(2)}) collective-permute-start(bf16[512,768]{1,0:T(8,128)(2,1)} %param.10), channel_id=1, source_target_pairs={{0,16},{16,0},{1,17},{17,1},{2,18},{18,2},{3,19},{19,3},{4,20},{20... | collective-permute-start | bytes 2359304 | tf_op jit(solution)/shard_map/ppermute | solution.py:211
  13.2 179.1 %collective-permute-start.1 = (bf16[1920,768]{1,0:T(8,128)(2,1)}, bf16[1920,768]{1,0:T(8,128)(2,1)}, u32[]{:S(2)}, u32[]{:S(2)}) collective-permute-start(bf16[1920,768]{1,0:T(8,128)(2,1)} %pad_maximum_fusion.12), channel_id=1, source_target_pairs={{0,0},{1,8},{2,4},{3,12},{4,2},{5,10},{6,6},{7,14},{8,1},{9,9},{10... | collective-permute-start | bytes 8847368 | tf_op jit(solution)/shard_map/ppermute | solution.py:218
  120.8 328.2 %reduce-scatter.10.cloned.1.call-start = ((), (), s32[]{:S(2)}) async-start(), calls=%async_computation.6 | async-start | bytes 11796480 | tf_op jit(solution)/shard_map/reduce_scatter | solution.py:311
  192.3 35.8 %collective-permute-start.3 = (bf16[1920,768]{1,0:T(8,128)(2,1)}, bf16[1920,768]{1,0:T(8,128)(2,1)}, u32[]{:S(2)}, u32[]{:S(2)}) collective-permute-start(bf16[1920,768]{1,0:T(8,128)(2,1)} %collective-permute-done.1), channel_id=1, source_target_pairs={{0,8},{4,12},{8,0},{12,4},{1,9},{5,13},{9,1},{13,5},{2,10},{6,14},... | collective-permute-start | bytes 8847368 | tf_op jit(solution)/shard_map/ppermute | solution.py:211
  197.2 54.2 %collective-permute-start = (bf16[512,3072]{1,0:T(8,128)(2,1)}, bf16[512,3072]{1,0:T(8,128)(2,1)}, u32[]{:S(2)}, u32[]{:S(2)}) collective-permute-start(bf16[512,3072]{1,0:T(8,128)(2,1)} %pad_maximum_fusion.9), channel_id=1, source_target_pairs={{0,16},{16,0},{1,17},{17,1},{2,18},{18,2},{3,19},{19,3},{4,20},{20... | collective-permute-start | bytes 9437192 | tf_op jit(solution)/shard_map/ppermute | solution.py:211
  215.5 86.7 %collective-permute-start.11 = (bf16[512,3072]{1,0:T(8,128)(2,1)}, bf16[512,3072]{1,0:T(8,128)(2,1)}, u32[]{:S(2)}, u32[]{:S(2)}) collective-permute-start(bf16[512,3072]{1,0:T(8,128)(2,1)} %pad_maximum_fusion.11), channel_id=1, source_target_pairs={{0,16},{16,0},{1,17},{17,1},{2,18},{18,2},{3,19},{19,3},{4,20},{20... | collective-permute-start | bytes 9437192 | tf_op jit(solution)/shard_map/ppermute | solution.py:211
  217.0 24.4 %collective-permute-start.2 = (bf16[1920,768]{1,0:T(8,128)(2,1)}, bf16[1920,768]{1,0:T(8,128)(2,1)}, u32[]{:S(2)}, u32[]{:S(2)}) collective-permute-start(bf16[1920,768]{1,0:T(8,128)(2,1)} %collective-permute-done.1), channel_id=1, source_target_pairs={{0,4},{4,0},{8,12},{12,8},{1,5},{5,1},{9,13},{13,9},{2,6},{6,2},{1... | collective-permute-start | bytes 8847368 | tf_op jit(solution)/shard_map/ppermute | solution.py:211
  228.1 16.7 %collective-permute-start.4 = (bf16[1920,768]{1,0:T(8,128)(2,1)}, bf16[1920,768]{1,0:T(8,128)(2,1)}, u32[]{:S(2)}, u32[]{:S(2)}) collective-permute-start(bf16[1920,768]{1,0:T(8,128)(2,1)} %collective-permute-done.3), channel_id=1, source_target_pairs={{0,4},{4,0},{8,12},{12,8},{1,5},{5,1},{9,13},{13,9},{2,6},{6,2},{1... | collective-permute-start | bytes 8847368 | tf_op jit(solution)/shard_map/ppermute | solution.py:211
  235.8 138.6 %collective-permute-start.5 = (bf16[768,2688]{1,0:T(8,128)(2,1)}, bf16[768,2688]{1,0:T(8,128)(2,1)}, u32[]{:S(2)}, u32[]{:S(2)}) collective-permute-start(bf16[768,2688]{1,0:T(8,128)(2,1)} %pad_maximum_fusion.4), channel_id=1, source_target_pairs={{0,0},{1,8},{2,4},{3,12},{4,2},{5,10},{6,6},{7,14},{8,1},{9,9},{10... | collective-permute-start | bytes 12386312 | tf_op jit(solution)/shard_map/ppermute | solution.py:218
  241.4 60.9 %copy-start.3 = (bf16[512,768]{1,0:T(8,128)(2,1)S(1)}, bf16[512,768]{1,0:T(8,128)(2,1)}, u32[]{:S(2)}) copy-start(bf16[512,768]{1,0:T(8,128)(2,1)} %copy-done.2) | copy-start | bytes 2359300
  241.4 60.9 %copy-start.5 = (bf16[512,768]{1,0:T(8,128)(2,1)S(1)}, bf16[512,768]{1,0:T(8,128)(2,1)}, u32[]{:S(2)}) copy-start(bf16[512,768]{1,0:T(8,128)(2,1)} %copy-done.4) | copy-start | bytes 2359300
  241.4 60.9 %copy-start.7 = (bf16[512,768]{1,0:T(8,128)(2,1)S(1)}, bf16[512,768]{1,0:T(8,128)(2,1)}, u32[]{:S(2)}) copy-start(bf16[512,768]{1,0:T(8,128)(2,1)} %copy-done.6) | copy-start | bytes 2359300
  241.4 60.9 %copy-start.9 = (bf16[512,768]{1,0:T(8,128)(2,1)S(1)}, bf16[512,768]{1,0:T(8,128)(2,1)}, u32[]{:S(2)}) copy-start(bf16[512,768]{1,0:T(8,128)(2,1)} %copy-done.8) | copy-start | bytes 2359300
  310.8 17.5 %copy-start.10 = (bf16[512,3072]{1,0:T(8,128)(2,1)S(1)}, bf16[512,3072]{1,0:T(8,128)(2,1)}, u32[]{:S(2)}) copy-start(bf16[512,3072]{1,0:T(8,128)(2,1)} %get-tuple-element.29) | copy-start | bytes 9437188
  374.5 265.3 %reduce-scatter.8.cloned.1.call-start = ((), (), s32[]{:S(2)}) async-start(), calls=%async_computation.5 | async-start | bytes 11796480 | tf_op jit(solution)/shard_map/reduce_scatter | solution.py:273
  375.0 341.7 %reduce-scatter.12.cloned.1.call-start = ((), (), s32[]{:S(2)}) async-start(), calls=%async_computation.7 | async-start | bytes 8847360 | tf_op jit(solution)/shard_map/reduce_scatter | solution.py:314
  386.7 14.1 %copy-start.11 = (bf16[512,3072]{1,0:T(8,128)(2,1)S(1)}, bf16[512,3072]{1,0:T(8,128)(2,1)}, u32[]{:S(2)}) copy-start(bf16[512,3072]{1,0:T(8,128)(2,1)} %get-tuple-element.29) | copy-start | bytes 9437188
  449.1 458.3 %reduce-scatter.16.cloned.1.call-start = ((), (), s32[]{:S(2)}) async-start(), calls=%async_computation.11 | async-start | bytes 2949120
  449.3 142.0 %collective-permute-start.7 = (bf16[768,2688]{1,0:T(8,128)(2,1)}, bf16[768,2688]{1,0:T(8,128)(2,1)}, u32[]{:S(2)}, u32[]{:S(2)}) collective-permute-start(bf16[768,2688]{1,0:T(8,128)(2,1)} %collective-permute-done.5), channel_id=1, source_target_pairs={{0,8},{4,12},{8,0},{12,4},{1,9},{5,13},{9,1},{13,5},{2,10},{6,14},... | collective-permute-start | bytes 12386312 | tf_op jit(solution)/shard_map/ppermute | solution.py:211
  451.1 151.2 %collective-permute-start.6 = (bf16[768,2688]{1,0:T(8,128)(2,1)}, bf16[768,2688]{1,0:T(8,128)(2,1)}, u32[]{:S(2)}, u32[]{:S(2)}) collective-permute-start(bf16[768,2688]{1,0:T(8,128)(2,1)} %collective-permute-done.5), channel_id=1, source_target_pairs={{0,4},{4,0},{8,12},{12,8},{1,5},{5,1},{9,13},{13,9},{2,6},{6,2},{1... | collective-permute-start | bytes 12386312 | tf_op jit(solution)/shard_map/ppermute | solution.py:211
  591.3 17.2 %collective-permute-start.8 = (bf16[768,2688]{1,0:T(8,128)(2,1)}, bf16[768,2688]{1,0:T(8,128)(2,1)}, u32[]{:S(2)}, u32[]{:S(2)}) collective-permute-start(bf16[768,2688]{1,0:T(8,128)(2,1)} %collective-permute-done.7), channel_id=1, source_target_pairs={{0,4},{4,0},{8,12},{12,8},{1,5},{5,1},{9,13},{13,9},{2,6},{6,2},{1... | collective-permute-start | bytes 12386312 | tf_op jit(solution)/shard_map/ppermute | solution.py:211
  593.2 21.7 %copy-start.15 = (bf16[768,1536]{1,0:T(8,128)(2,1)}, bf16[768,1536]{1,0:T(8,128)(2,1)S(1)}, u32[]{:S(2)}) copy-start(bf16[768,1536]{1,0:T(8,128)(2,1)S(1)} %slice.96) | copy-start | bytes 7077892
  596.1 31.5 %copy-start.17 = (bf16[768,1152]{1,0:T(8,128)(2,1)}, bf16[768,1152]{1,0:T(8,128)(2,1)S(1)}, u32[]{:S(2)}) copy-start(bf16[768,1152]{1,0:T(8,128)(2,1)S(1)} %slice.88) | copy-start | bytes 5308420
  598.6 16.3 %copy-start.16 = (bf16[768,1536]{1,0:T(8,128)(2,1)}, bf16[768,1536]{1,0:T(8,128)(2,1)S(1)}, u32[]{:S(2)}) copy-start(bf16[768,1536]{1,0:T(8,128)(2,1)S(1)} %slice.98) | copy-start | bytes 7077892
  638.2 70.6 %collective-permute-start.9 = (bf16[512,3072]{1,0:T(8,128)(2,1)}, bf16[512,3072]{1,0:T(8,128)(2,1)}, u32[]{:S(2)}, u32[]{:S(2)}) collective-permute-start(bf16[512,3072]{1,0:T(8,128)(2,1)} %add_convert_fusion.1), channel_id=1, source_target_pairs={{0,16},{16,0},{1,17},{17,1},{2,18},{18,2},{3,19},{19,3},{4,20},{20... | collective-permute-start | bytes 9437192 | tf_op jit(solution)/shard_map/ppermute | solution.py:211
  644.0 263.4 %reduce-scatter.14.cloned.1.call-start = ((), (), s32[]{:S(2)}) async-start(), calls=%async_computation.8 | async-start | bytes 3932160 | tf_op jit(solution)/shard_map/reduce_scatter | solution.py:342
  716.7 196.7 %copy-start.1 = (bf16[1024,1536]{1,0:T(8,128)(2,1)S(1)}, bf16[1024,1536]{1,0:T(8,128)(2,1)}, u32[]{:S(2)}) copy-start(bf16[1024,1536]{1,0:T(8,128)(2,1)} %param.12) | copy-start | bytes 9437188
  716.7 171.7 %collective-permute-start.13 = (bf16[768,1536]{1,0:T(8,128)(2,1)}, bf16[768,1536]{1,0:T(8,128)(2,1)}, u32[]{:S(2)}, u32[]{:S(2)}) collective-permute-start(bf16[768,1536]{1,0:T(8,128)(2,1)} %reduce-scatter.10.cloned.1.call-done), channel_id=1, source_target_pairs={{0,0},{1,8},{2,4},{3,12},{4,2},{5,10},{6,6},{7,14},{8,1},{9,9},{10... | collective-permute-start | bytes 7077896 | tf_op jit(solution)/shard_map/ppermute | solution.py:218
  722.3 185.1 %collective-permute-start.12 = (bf16[768,1152]{1,0:T(8,128)(2,1)}, bf16[768,1152]{1,0:T(8,128)(2,1)}, u32[]{:S(2)}, u32[]{:S(2)}) collective-permute-start(bf16[768,1152]{1,0:T(8,128)(2,1)} %reduce-scatter.12.cloned.1.call-done), channel_id=1, source_target_pairs={{0,0},{1,8},{2,4},{3,12},{4,2},{5,10},{6,6},{7,14},{8,1},{9,9},{10... | collective-permute-start | bytes 5308424 | tf_op jit(solution)/shard_map/ppermute | solution.py:218
  (9 other events, 41.4 us)
Sparse Core Ops, SparseCore 0:
  9.6 111.1 all-gather.4
  122.4 89.0 all-gather.6
  374.6 74.4 reduce-scatter.9
  452.1 129.0 reduce-scatter.7
  583.5 67.5 reduce-scatter.11
  654.2 33.0 reduce-scatter.15
  716.9 151.1 reduce-scatter.13

commit v3 on v2

--- a/solution.py
+++ b/solution.py
@@ -222,8 +222,31 @@
     return lax.optimization_barrier((value,) + earlier)[0]
 
 
-def four_parts(block):
-    opposite = exchange(block, "gy", 2)
+def at_place(parts, index, axis):
+    taken = [lax.dynamic_index_in_dim(part, index, axis, keepdims=False) for part in parts]
+    return taken[0] if len(taken) == 1 else jnp.concatenate(taken, axis=taken[0].ndim - 2)
+
+
+def add(left, right):
+    return (left.astype(jnp.float32) + right.astype(jnp.float32)).astype(jnp.bfloat16)
+
+
+def pair_sum(parts):
+    core = lax.rem(lax.axis_index("gy"), 2)
+    pairs = [part.reshape(2, 2, part.shape[0] // 4, part.shape[1]) for part in parts]
+    arrived = exchange(at_place(pairs, 1 - core, 1), "gy", 1)
+    return add(at_place(pairs, core, 1), arrived)
+
+
+def far_sum(pair, *earlier):
+    row = lax.axis_index("gy") // 2
+    sent = lax.dynamic_index_in_dim(pair, 1 - row, 0, keepdims=False)
+    arrived = exchange(after(sent, *earlier) if earlier else sent, "gy", 2)
+    return add(lax.dynamic_index_in_dim(pair, row, 0, keepdims=False), arrived)
+
+
+def four_parts(block, *earlier):
+    opposite = exchange(after(block, *earlier), "gy", 2)
     beside = exchange(block, "gy", 1)
     return block, beside, opposite, exchange(opposite, "gy", 1)
 
@@ -254,7 +277,8 @@
     units = hidden_in.shape[1]
 
     grad_blocks = lax.all_gather(out_grad, "gz", axis=0)
-    turned_out = turn(jnp.concatenate([hidden_out, attend_out], axis=0))
+    out_block = jnp.concatenate([hidden_out, attend_out], axis=0)
+    turned_out = turn(after(out_block, grad_blocks))
     grad_own = both_halves(out_grad)
     activated = gelu_value(hidden_pre.astype(jnp.float32)).astype(jnp.bfloat16)
     part_attend_out = jnp.einsum(
@@ -263,19 +287,8 @@
     part_hidden_out = jnp.einsum(
         "tg,td->gd", activated, grad_own, preferred_element_type=jnp.float32
     ).astype(jnp.bfloat16)
-
-    normed_blocks = lax.all_gather(
-        after(normed, grad_blocks, part_attend_out, part_hidden_out), "gz", axis=0
-    )
-    out_parts = four_parts(turned_out)
-    in_block = jnp.concatenate([hidden_in, attend_in], axis=1)
-    turned_in = turn(after(in_block, out_parts[2]))
-    hidden_out_grad = lax.psum_scatter(
-        after(part_hidden_out, normed_blocks), "gy", scatter_dimension=0, tiled=True
-    )
-    attend_out_grad = lax.psum_scatter(
-        after(part_attend_out, hidden_out_grad), "gy", scatter_dimension=0, tiled=True
-    )
+    out_sum = far_sum(pair_sum([part_hidden_out, part_attend_out]))
+    hidden_out_grad, attend_out_grad = out_sum[:units], out_sum[units:]
 
     order = []
     for flip in range(4):
@@ -286,6 +299,10 @@
             [lax.dynamic_index_in_dim(grad_blocks, at, 0, keepdims=False) for at in order], axis=1
         )
     )
+    out_parts = four_parts(turned_out, out_sum, grad_slab)
+    normed_blocks = lax.all_gather(after(normed, turned_out, grad_slab), "gz", axis=0)
+    in_block = jnp.concatenate([hidden_in, attend_in], axis=1)
+    turned_in = turn(after(in_block, out_parts[2]))
     normed_slab = both_halves(jnp.concatenate([normed_blocks[at] for at in SWAP], axis=1))
     hidden_rows = jnp.concatenate([part[:units] for part in out_parts], axis=1)
     attend_rows = jnp.concatenate([part[units:] for part in out_parts], axis=1)
@@ -296,7 +313,7 @@
     )
     hidden_grad = (hidden_part * gelu_slope(pre_here.astype(jnp.float32))).astype(jnp.bfloat16)
     part_hidden_in = jnp.einsum(
-        "td,tq->dq", normed_slab, hidden_grad, preferred_element_type=jnp.float32
+        "td,tq->dq", normed_slab, after(hidden_grad, turned_in), preferred_element_type=jnp.float32
     ).astype(jnp.bfloat16)
 
     head_grad = jnp.einsum(
@@ -308,16 +325,17 @@
         "td,tq->dq", normed_slab, projected_grad, preferred_element_type=jnp.float32
     ).astype(jnp.bfloat16)
 
-    hidden_in_sum = lax.psum_scatter(
-        after(part_hidden_in, attend_out_grad, turned_in), "gy", scatter_dimension=0, tiled=True
-    )
-    attend_in_sum = lax.psum_scatter(
-        after(part_attend_in, hidden_in_sum), "gy", scatter_dimension=0, tiled=True
-    )
+    hidden_in_sum = far_sum(pair_sum([part_hidden_in]))
     hidden_in_grad = turn(hidden_in_sum)
+    far_in = exchange(after(turned_in, hidden_in_sum), "gy", 2)
+    in_parts = (
+        turned_in,
+        exchange(turned_in, "gy", 1),
+        far_in,
+        exchange(after(far_in, hidden_in_grad), "gy", 1),
+    )
+    attend_in_sum = far_sum(pair_sum([part_attend_in]), in_parts[2])
     attend_in_grad = turn(attend_in_sum)
-
-    in_parts = four_parts(turned_in)
     hidden_cols = jnp.concatenate([part[:, :units] for part in in_parts], axis=0)
     attend_cols = jnp.concatenate([part[:, units:] for part in in_parts], axis=0)
 
@@ -328,7 +346,8 @@
             "tq,dq->td", attend_part, attend_cols, preferred_element_type=jnp.float32
         ) + jnp.einsum("tq,dq->td", hidden_part, hidden_cols, preferred_element_type=jnp.float32)
 
-    arrived = exchange(input_grad((1 - side) * half).astype(jnp.bfloat16), "gx", 1)
+    leaving = input_grad((1 - side) * half).astype(jnp.bfloat16)
+    arrived = exchange(leaving, "gx", 1)
     row_grad = (input_grad(side * half) + arrived.astype(jnp.float32)).astype(jnp.bfloat16)
     row_grad = jnp.concatenate(
         [
@@ -340,7 +359,7 @@
         axis=1,
     )
     normed_grad = lax.psum_scatter(
-        after(row_grad, attend_in_sum), "gz", scatter_dimension=1, tiled=True
+        after(row_grad, attend_in_grad), "gz", scatter_dimension=1, tiled=True
     )
     return normed_grad, attend_in_grad, hidden_in_grad, attend_out_grad, hidden_out_grad
 

time: 933 us -> 942 us (level)
  waiting for transfers between devices: 668 us -> 593 us
  local copies, waits for them, and re-layouts: 61.2 us -> 103 us
  other arithmetic: 29.6 us -> 56.7 us
  starting transfers between devices: 20.5 us -> 35.6 us
    ppermute x4, waiting for transfers between devices: 286 us -> 158 us  [turn(): return lax.ppermute(block, ('gy', 'gz'), pairs)]
    ppermute x10 -> x16, waiting for transfers between devices: 260 us -> 317 us  [exchange(): return lax.ppermute(block, axis, [(i, i ^ flip) for i in range(size)])]
    convert_element_type x0 -> x6, other arithmetic: none -> 23.3 us  [add(): (left.astype(jnp.float32) + right.astype(jnp.float32)).astype(jnp.bfloat16)]
    ppermute x10 -> x16, starting transfers between devices: 6.35 us -> 27.3 us  [exchange(): return lax.ppermute(block, axis, [(i, i ^ flip) for i in range(size)])]
    dynamic_slice x0 -> x3, local copies, waits for them, and re-layouts: none -> 17.3 us  [at_place(): lax.dynamic_index_in_dim(part, index, axis, keepdims=False)]
    squeeze x0 -> x6, local copies, waits for them, and re-layouts: none -> 15.1 us  [the longest x3 10.4 us: at_place(): lax.dynamic_index_in_dim(part, index, axis, keepdims=False)]
    reduce_scatter x4 -> x1, waiting for transfers between devices: 38 us -> 52.5 us  [local_columns(): lax.psum_scatter(after(row_grad, attend_in_grad), 'gz', scatter_dimension...]
    all_gather x1, waiting for transfers between devices: 14.2 us -> 0.02 us  [local_columns(): lax.all_gather(after(normed, turned_out, grad_slab), 'gz', axis=0)]
  transfers between devices with their start and end apart: 21 -> 23, of which waited for: 13 -> 15; matrix products, arithmetic and copies ran while one was open for 21% -> 20% of each run, Pallas kernels for 2% -> 2%
where the time goes in v3:
time: 942 us; the launch traced here: 926 us
  waiting for transfers between devices  593 us (63%)
  matrix products  109 us (12%)
  local copies, waits for them, and re-layouts  103 us (11%)
  other arithmetic  56.7 us (6%)
  starting transfers between devices  35.6 us (4%)
  between operations  14.7 us (2%)
  Pallas kernels  14.1 us (1%)
    ppermute x16, waiting for transfers between devices, exchange(): return lax.ppermute(block, axis, [(i, i ^ flip) for i in range(size)])  317 us
    ppermute x4, waiting for transfers between devices, turn(): return lax.ppermute(block, ('gy', 'gz'), pairs)  158 us
    all_gather x1, waiting for transfers between devices, local_columns(): grad_blocks = lax.all_gather(out_grad, 'gz', axis=0)  64.5 us
    reduce_scatter x1, waiting for transfers between devices, local_columns(): lax.psum_scatter(after(row_grad, attend_in_grad), 'gz', scatter_dimension...  52.5 us
    ppermute x16, starting transfers between devices, exchange(): return lax.ppermute(block, axis, [(i, i ^ flip) for i in range(size)])  27.3 us
    dot_general x2, matrix products, input_grad(): jnp.einsum('tq,dq->td', hidden_part, hidden_cols, preferred_element_type=...  23.4 us
    convert_element_type x6, other arithmetic, add(): (left.astype(jnp.float32) + right.astype(jnp.float32)).astype(jnp.bfloat16)  23.3 us
    dot_general x2, matrix products, input_grad(): jnp.einsum('tq,dq->td', attend_part, attend_cols, preferred_element_type=...  22.4 us
  transfers between devices with their start and end apart: 23, of which 15 were waited for; matrix products, arithmetic and copies ran while one was open for 20% of the time, Pallas kernels for 2%

profile of v3, /device:TPU:4, one launch (start us, length us, event | category | flops | bytes accessed | tf_op | source)
XLA Modules:
  0.0 926.3 jit_solution(15204300409170626660)
XLA Ops:
  8.8 18.1 %collective-permute-done.3 = bf16[512,768]{1,0:T(8,128)(2,1)} collective-permute-done((bf16[512,768]{1,0:T(8,128)(2,1)}, bf16[512,768]{1,0:T(8,128)(2,1)}, u32[]{:S(2)}, u32[]{:S(2)}) %collective-permute-start.3) | collective-permute-done | bytes 786464 | tf_op jit(solution)/shard_map/ppermute | solution.py:211
  28.4 16.5 %fusion.6 = bf16[6144,768]{1,0:T(8,128)(2,1)} fusion(bf16[1024,6144]{1,0:T(8,128)(2,1)} %param.13, bf16[512,768]{1,0:T(8,128)(2,1)S(1)} %get-tuple-element.44, bf16[512,768]{1,0:T(8,128)(2,1)S(1)} %get-tuple-element.43), kind=kOutput, calls=%fused_computation.14 | convolution fusion | flops 9709289472 | bytes 23592960 | tf_op jit(solution)/shard_map/tg,td->gd/dot_general | solution.py:287
  53.7 8.1 dynamic-slice_bitcast_fusion.2
  61.7 7.0 constant_dynamic-slice_fusion.5
  68.8 5.4 copy.15
  74.2 5.3 pad_maximum_fusion.4
  80.0 64.5 %all-gather.5.cloned.1.call-done = bf16[2048,768]{1,0:T(8,128)(2,1)} async-done(((bf16[512,768]{1,0:T(8,128)(2,1)}), bf16[2048,768]{1,0:T(8,128)(2,1)}) %all-gather.5.cloned.1.call-update) | async-done | bytes 3145744 | tf_op jit(solution)/shard_map/all_gather | solution.py:279
  161.2 5.5 add_convert_fusion
  171.0 22.3 %collective-permute-start.5 = (bf16[1920,768]{1,0:T(8,128)(2,1)}, bf16[1920,768]{1,0:T(8,128)(2,1)}, u32[]{:S(2)}, u32[]{:S(2)}) collective-permute-start(bf16[1920,768]{1,0:T(8,128)(2,1)} %dynamic-slice_bitcast_fusion.4), channel_id=1, source_target_pairs={{0,8},{4,12},{8,0},{12,4},{1,9},{5,13},{9,1},{13,5},{2,10},{6,14},... | collective-permute-start | bytes 8847368 | tf_op jit(solution)/shard_map/ppermute | solution.py:211
  193.4 26.1 %collective-permute-done = bf16[512,3072]{1,0:T(8,128)(2,1)} collective-permute-done((bf16[512,3072]{1,0:T(8,128)(2,1)}, bf16[512,3072]{1,0:T(8,128)(2,1)}, u32[]{:S(2)}, u32[]{:S(2)}) %collective-permute-start) | collective-permute-done | bytes 3145760 | tf_op jit(solution)/shard_map/ppermute | solution.py:211
  224.2 35.8 %collective-permute-done.1 = bf16[1920,768]{1,0:T(8,128)(2,1)} collective-permute-done((bf16[1920,768]{1,0:T(8,128)(2,1)}, bf16[1920,768]{1,0:T(8,128)(2,1)}, u32[]{:S(2)}, u32[]{:S(2)}) %collective-permute-start.1) | collective-permute-done | bytes 2949152 | tf_op jit(solution)/shard_map/ppermute | solution.py:218
  260.1 39.2 %collective-permute-done.5 = bf16[1920,768]{1,0:T(8,128)(2,1)} collective-permute-done((bf16[1920,768]{1,0:T(8,128)(2,1)}, bf16[1920,768]{1,0:T(8,128)(2,1)}, u32[]{:S(2)}, u32[]{:S(2)}) %collective-permute-start.5) | collective-permute-done | bytes 2949152 | tf_op jit(solution)/shard_map/ppermute | solution.py:211
  299.3 5.1 fusion.27
  304.4 56.1 %collective-permute-done.6 = bf16[1920,768]{1,0:T(8,128)(2,1)} collective-permute-done((bf16[1920,768]{1,0:T(8,128)(2,1)}, bf16[1920,768]{1,0:T(8,128)(2,1)}, u32[]{:S(2)}, u32[]{:S(2)}) %collective-permute-start.6) | collective-permute-done | bytes 2949152 | tf_op jit(solution)/shard_map/ppermute | solution.py:211
  382.3 17.4 %fusion.26 = bf16[1024,1536]{1,0:T(8,128)(2,1)} fusion(bf16[1536,768]{1,0:T(8,128)(2,1)} %slice.105, bf16[1536,768]{1,0:T(8,128)(2,1)} %slice.104, bf16[1536,768]{1,0:T(8,128)(2,1)} %slice.103, bf16[1536,768]{1,0:T(8,128)(2,1)} %slice.102, bf16[1024,6144]{1,0:T(8,128)(2,1)} %param.13, s32[]{:T(128)S(6)} %select_n.143, ...), kind=kOutput, calls=%fused_computation.40 | convolution fusion | flops 9731309568 | bytes 22020100 | tf_op jit(solution)/shard_map/td,gd->tg/dot_general | solution.py:311
  399.7 40.2 %collective-permute-done.10 = bf16[512,3072]{1,0:T(8,128)(2,1)} collective-permute-done((bf16[512,3072]{1,0:T(8,128)(2,1)}, bf16[512,3072]{1,0:T(8,128)(2,1)}, u32[]{:S(2)}, u32[]{:S(2)}) %collective-permute-start.10) | collective-permute-done | bytes 3145760 | tf_op jit(solution)/shard_map/ppermute | solution.py:211
  444.7 56.5 %collective-permute-done.8 = bf16[768,2688]{1,0:T(8,128)(2,1)} collective-permute-done((bf16[768,2688]{1,0:T(8,128)(2,1)}, bf16[768,2688]{1,0:T(8,128)(2,1)}, u32[]{:S(2)}, u32[]{:S(2)}) %collective-permute-start.8) | collective-permute-done | bytes 4128800 | tf_op jit(solution)/shard_map/ppermute | solution.py:218
  501.2 13.3 %convolution_convert_fusion.1 = bf16[3072,1536]{1,0:T(8,128)(2,1)S(1)} fusion(bf16[1024,1536]{1,0:T(8,128)(2,1)} %fusion.26, bf16[512,3072]{1,0:T(8,128)(2,1)} %get-tuple-element.26, bf16[512,3072]{1,0:T(8,128)(2,1)} %get-tuple-element.25), kind=kOutput, calls=%fused_computation.9 | convolution fusion | flops 9680977920 | bytes 18874368 | tf_op jit(solution)/shard_map/td,tq->dq/dot_general | solution.py:315
  514.9 8.0 collective-permute-done.11
  537.5 46.3 %collective-permute-done.12 = bf16[768,1536]{1,0:T(8,128)(2,1)S(1)} collective-permute-done((bf16[768,1536]{1,0:T(8,128)(2,1)}, bf16[768,1536]{1,0:T(8,128)(2,1)S(1)}, u32[]{:S(2)}, u32[]{:S(2)}) %collective-permute-start.12) | collective-permute-done | bytes 2359328 | tf_op jit(solution)/shard_map/ppermute | solution.py:211
  589.8 14.1 %shard_map.128 = bf16[1024,1152]{1,0:T(8,128)(2,1)S(1)} custom-call(bf16[1024,1152]{1,0:T(8,128)(2,1)S(1)} %constant_dynamic-slice_fusion.6.keyed_ref, bf16[1024,384]{1,0:T(8,128)(2,1)S(1)} %fusion.45.grad_ref), custom_call_target="tpu_custom_call" | custom-call | flops 4026531840 | bytes 5505024 | tf_op jit(solution)/shard_map/pallas_call | solution.py:191
  605.9 9.1 convolution_convert_fusion
  620.3 65.8 %collective-permute-done.14 = bf16[768,1536]{1,0:T(8,128)(2,1)S(1)} collective-permute-done((bf16[768,1536]{1,0:T(8,128)(2,1)S(1)}, bf16[768,1536]{1,0:T(8,128)(2,1)S(1)}, u32[]{:S(2)}, u32[]{:S(2)}) %collective-permute-start.14) | collective-permute-done | bytes 2359328 | tf_op jit(solution)/shard_map/ppermute | solution.py:218
  687.5 39.8 %collective-permute-done.13 = bf16[768,2688]{1,0:T(8,128)(2,1)} collective-permute-done((bf16[768,2688]{1,0:T(8,128)(2,1)}, bf16[768,2688]{1,0:T(8,128)(2,1)}, u32[]{:S(2)}, u32[]{:S(2)}) %collective-permute-start.13) | collective-permute-done | bytes 4128800 | tf_op jit(solution)/shard_map/ppermute | solution.py:211
  752.2 12.4 %fusion.41 = f32[512,3072]{1,0:T(8,128)} fusion(bf16[768,1536]{1,0:T(8,128)(2,1)} %slice.111, bf16[768,1536]{1,0:T(8,128)(2,1)} %slice.110, bf16[768,1536]{1,0:T(8,128)(2,1)S(1)} %slice.109, bf16[768,1536]{1,0:T(8,128)(2,1)S(1)} %slice.108, bf16[1024,1536]{1,0:T(8,128)(2,1)} %fusion.26, s32[]{:T(128)S(6)} %select_n.144), kind=kOutput, calls=%fused_computation.74 | convolution fusion | flops 4869586944 | bytes 17301508 | tf_op jit(solution)/shard_map/tq,dq->td/dot_general | solution.py:347
  766.3 12.1 %add_convert_fusion.2 = bf16[512,3072]{1,0:T(8,128)(2,1)} fusion(f32[512,3072]{1,0:T(8,128)} %fusion.41, bf16[768,1152]{1,0:T(8,128)(2,1)S(1)} %slice.107, bf16[768,1152]{1,0:T(8,128)(2,1)} %slice.106, bf16[768,1152]{1,0:T(8,128)(2,1)} %slice.97, bf16[768,1152]{1,0:T(8,128)(2,1)S(1)} %slice.96, bf16[1024,1152]{1,0:T(8,128)(2,1)S(1)} %shard_map.128, ...), kind=kOutput, calls=%fused_computation.39 | convolution fusion | flops 3655335936 | bytes 17694724 | tf_op jit(solution)/shard_map/tq,dq->td/dot_general | solution.py:345
  778.8 5.5 collective-permute-done.18
  789.9 11.0 %fusion.42 = f32[512,3072]{1,0:T(8,128)S(1)} fusion(bf16[768,1536]{1,0:T(8,128)(2,1)} %slice.111, bf16[768,1536]{1,0:T(8,128)(2,1)} %slice.110, bf16[768,1536]{1,0:T(8,128)(2,1)} %copy-done.21, bf16[768,1536]{1,0:T(8,128)(2,1)} %copy-done.20, bf16[1024,1536]{1,0:T(8,128)(2,1)} %fusion.26, s32[]{:T(128)S(6)} %select_n.140), kind=kOutput, calls=%fused_computation.75 | convolution fusion | flops 4869586944 | bytes 17301508 | tf_op jit(solution)/shard_map/tq,dq->td/dot_general | solution.py:347
  800.9 10.3 %fusion.48 = f32[512,3072]{1,0:T(8,128)} fusion(bf16[768,1152]{1,0:T(8,128)(2,1)} %copy-done.24, bf16[768,1152]{1,0:T(8,128)(2,1)} %slice.106, bf16[768,1152]{1,0:T(8,128)(2,1)} %slice.97, bf16[768,1152]{1,0:T(8,128)(2,1)} %copy-done.23, bf16[1024,1152]{1,0:T(8,128)(2,1)S(1)} %shard_map.128, s32[]{:T(128)S(6)} %select_n.140), kind=kOutput, calls=%fused_computation.80 | convolution fusion | flops 3652190208 | bytes 14548996 | tf_op jit(solution)/shard_map/tq,dq->td/dot_general | solution.py:345
  811.2 38.1 %collective-permute-done.16 = bf16[512,3072]{1,0:T(8,128)(2,1)} collective-permute-done((bf16[512,3072]{1,0:T(8,128)(2,1)}, bf16[512,3072]{1,0:T(8,128)(2,1)}, u32[]{:S(2)}, u32[]{:S(2)}) %collective-permute-start.16) | collective-permute-done | bytes 3145760 | tf_op jit(solution)/shard_map/ppermute | solution.py:211
  849.2 5.5 add_convert_fusion.1
  862.5 52.5 %reduce-scatter.2.cloned.1.call-done = bf16[512,768]{1,0:T(8,128)(2,1)} async-done(((bf16[512,3072]{1,0:T(8,128)(2,1)}), bf16[512,768]{1,0:T(8,128)(2,1)}) %reduce-scatter.2.cloned.1.call-update) | async-done | bytes 786448 | tf_op jit(solution)/shard_map/reduce_scatter | solution.py:361
  (130 shorter events, 138.9 us)
Async XLA Ops:
  7.2 37.7 %copy-start = (bf16[1024,1536]{1,0:T(8,128)(2,1)S(1)}, bf16[1024,1536]{1,0:T(8,128)(2,1)}, u32[]{:S(2)}) copy-start(bf16[1024,1536]{1,0:T(8,128)(2,1)} %param.12) | copy-start | bytes 9437188
  7.2 137.3 %all-gather.5.cloned.1.call-start = ((), (), s32[]{:S(2)}) async-start(), calls=%async_computation.2 | async-start | bytes 3932160 | tf_op jit(solution)/shard_map/all_gather | solution.py:279
  7.2 19.7 %collective-permute-start.3 = (bf16[512,768]{1,0:T(8,128)(2,1)}, bf16[512,768]{1,0:T(8,128)(2,1)}, u32[]{:S(2)}, u32[]{:S(2)}) collective-permute-start(bf16[512,768]{1,0:T(8,128)(2,1)} %param.10), channel_id=1, source_target_pairs={{0,16},{16,0},{1,17},{17,1},{2,18},{18,2},{3,19},{19,3},{4,20},{20... | collective-permute-start | bytes 2359304 | tf_op jit(solution)/shard_map/ppermute | solution.py:211
  79.5 81.8 %collective-permute-start.4 = (bf16[2,1920,768]{2,1,0:T(8,128)(2,1)}, bf16[2,1920,768]{2,1,0:T(8,128)(2,1)}, u32[]{:S(2)}, u32[]{:S(2)}) collective-permute-start(bf16[2,1920,768]{2,1,0:T(8,128)(2,1)} %pad_maximum_fusion.4), channel_id=1, source_target_pairs={{0,4},{4,0},{8,12},{12,8},{1,5},{5,1},{9,13},{13,9},{2,6},{6,2},{1... | collective-permute-start | bytes 17694728 | tf_op jit(solution)/shard_map/ppermute | solution.py:211
  79.5 285.3 %all-gather.7.cloned.1.call-start = ((), (), s32[]{:S(2)}) async-start(), calls=%async_computation.3 | async-start | bytes 3932160 | tf_op jit(solution)/shard_map/all_gather | solution.py:303
  149.3 70.1 %collective-permute-start = (bf16[512,3072]{1,0:T(8,128)(2,1)}, bf16[512,3072]{1,0:T(8,128)(2,1)}, u32[]{:S(2)}, u32[]{:S(2)}) collective-permute-start(bf16[512,3072]{1,0:T(8,128)(2,1)} %pad_maximum_fusion.8), channel_id=1, source_target_pairs={{0,16},{16,0},{1,17},{17,1},{2,18},{18,2},{3,19},{19,3},{4,20},{20... | collective-permute-start | bytes 9437192 | tf_op jit(solution)/shard_map/ppermute | solution.py:211
  159.3 100.7 %collective-permute-start.1 = (bf16[1920,768]{1,0:T(8,128)(2,1)}, bf16[1920,768]{1,0:T(8,128)(2,1)}, u32[]{:S(2)}, u32[]{:S(2)}) collective-permute-start(bf16[1920,768]{1,0:T(8,128)(2,1)} %pad_maximum_fusion.11), channel_id=1, source_target_pairs={{0,0},{1,8},{2,4},{3,12},{4,2},{5,10},{6,6},{7,14},{8,1},{9,9},{10... | collective-permute-start | bytes 8847368 | tf_op jit(solution)/shard_map/ppermute | solution.py:218
  169.3 50.2 %copy-start.9 = (bf16[512,768]{1,0:T(8,128)(2,1)S(1)}, bf16[512,768]{1,0:T(8,128)(2,1)}, u32[]{:S(2)}) copy-start(bf16[512,768]{1,0:T(8,128)(2,1)} %copy-done.8) | copy-start | bytes 2359300
  169.3 50.2 %copy-start.11 = (bf16[512,768]{1,0:T(8,128)(2,1)S(1)}, bf16[512,768]{1,0:T(8,128)(2,1)}, u32[]{:S(2)}) copy-start(bf16[512,768]{1,0:T(8,128)(2,1)} %copy-done.10) | copy-start | bytes 2359300
  169.3 50.2 %copy-start.13 = (bf16[512,768]{1,0:T(8,128)(2,1)S(1)}, bf16[512,768]{1,0:T(8,128)(2,1)}, u32[]{:S(2)}) copy-start(bf16[512,768]{1,0:T(8,128)(2,1)} %copy-done.12) | copy-start | bytes 2359300
  171.0 128.3 %collective-permute-start.5 = (bf16[1920,768]{1,0:T(8,128)(2,1)}, bf16[1920,768]{1,0:T(8,128)(2,1)}, u32[]{:S(2)}, u32[]{:S(2)}) collective-permute-start(bf16[1920,768]{1,0:T(8,128)(2,1)} %dynamic-slice_bitcast_fusion.4), channel_id=1, source_target_pairs={{0,8},{4,12},{8,0},{12,4},{1,9},{5,13},{9,1},{13,5},{2,10},{6,14},... | collective-permute-start | bytes 8847368 | tf_op jit(solution)/shard_map/ppermute | solution.py:211
  224.2 136.3 %copy-start.22 = (bf16[768,1536]{1,0:T(8,128)(2,1)S(1)}, bf16[768,1536]{1,0:T(8,128)(2,1)}, u32[]{:S(2)}) copy-start(bf16[768,1536]{1,0:T(8,128)(2,1)} %param.15) | copy-start | bytes 7077892
  260.0 655.0 %reduce-scatter.2.cloned.1.call-start = ((), (), s32[]{:S(2)}) async-start(), calls=%async_computation.1 | async-start | bytes 3932160 | tf_op jit(solution)/shard_map/reduce_scatter | solution.py:361
  260.1 100.5 %copy-start.25 = (bf16[768,1152]{1,0:T(8,128)(2,1)S(1)}, bf16[768,1152]{1,0:T(8,128)(2,1)}, u32[]{:S(2)}) copy-start(bf16[768,1152]{1,0:T(8,128)(2,1)} %param.14) | copy-start | bytes 5308420
  304.4 56.1 %collective-permute-start.6 = (bf16[1920,768]{1,0:T(8,128)(2,1)}, bf16[1920,768]{1,0:T(8,128)(2,1)}, u32[]{:S(2)}, u32[]{:S(2)}) collective-permute-start(bf16[1920,768]{1,0:T(8,128)(2,1)} %collective-permute-done.1), channel_id=1, source_target_pairs={{0,8},{4,12},{8,0},{12,4},{1,9},{5,13},{9,1},{13,5},{2,10},{6,14},... | collective-permute-start | bytes 8847368 | tf_op jit(solution)/shard_map/ppermute | solution.py:211
  304.4 68.2 %collective-permute-start.2 = (bf16[1920,768]{1,0:T(8,128)(2,1)}, bf16[1920,768]{1,0:T(8,128)(2,1)}, u32[]{:S(2)}, u32[]{:S(2)}) collective-permute-start(bf16[1920,768]{1,0:T(8,128)(2,1)} %collective-permute-done.1), channel_id=1, source_target_pairs={{0,4},{4,0},{8,12},{12,8},{1,5},{5,1},{9,13},{13,9},{2,6},{6,2},{1... | collective-permute-start | bytes 8847368 | tf_op jit(solution)/shard_map/ppermute | solution.py:211
  360.5 18.6 %collective-permute-start.7 = (bf16[1920,768]{1,0:T(8,128)(2,1)}, bf16[1920,768]{1,0:T(8,128)(2,1)}, u32[]{:S(2)}, u32[]{:S(2)}) collective-permute-start(bf16[1920,768]{1,0:T(8,128)(2,1)} %collective-permute-done.6), channel_id=1, source_target_pairs={{0,4},{4,0},{8,12},{12,8},{1,5},{5,1},{9,13},{13,9},{2,6},{6,2},{1... | collective-permute-start | bytes 8847368 | tf_op jit(solution)/shard_map/ppermute | solution.py:211
  362.7 138.5 %collective-permute-start.8 = (bf16[768,2688]{1,0:T(8,128)(2,1)}, bf16[768,2688]{1,0:T(8,128)(2,1)}, u32[]{:S(2)}, u32[]{:S(2)}) collective-permute-start(bf16[768,2688]{1,0:T(8,128)(2,1)} %pad_maximum_fusion.5), channel_id=1, source_target_pairs={{0,0},{1,8},{2,4},{3,12},{4,2},{5,10},{6,6},{7,14},{8,1},{9,9},{10... | collective-permute-start | bytes 12386312 | tf_op jit(solution)/shard_map/ppermute | solution.py:218
  368.7 71.1 %collective-permute-start.10 = (bf16[512,3072]{1,0:T(8,128)(2,1)}, bf16[512,3072]{1,0:T(8,128)(2,1)}, u32[]{:S(2)}, u32[]{:S(2)}) collective-permute-start(bf16[512,3072]{1,0:T(8,128)(2,1)} %pad_maximum_fusion.9), channel_id=1, source_target_pairs={{0,16},{16,0},{1,17},{17,1},{2,18},{18,2},{3,19},{19,3},{4,20},{20... | collective-permute-start | bytes 9437192 | tf_op jit(solution)/shard_map/ppermute | solution.py:211
  514.8 8.1 collective-permute-start.11
  530.3 53.5 %collective-permute-start.12 = (bf16[768,1536]{1,0:T(8,128)(2,1)}, bf16[768,1536]{1,0:T(8,128)(2,1)S(1)}, u32[]{:S(2)}, u32[]{:S(2)}) collective-permute-start(bf16[768,1536]{1,0:T(8,128)(2,1)} %dynamic-slice_bitcast_fusion.5), channel_id=1, source_target_pairs={{0,8},{4,12},{8,0},{12,4},{1,9},{5,13},{9,1},{13,5},{2,10},{6,14},... | collective-permute-start | bytes 7077896 | tf_op jit(solution)/shard_map/ppermute | solution.py:211
  534.3 52.1 %copy-start.14 = (bf16[512,3072]{1,0:T(8,128)(2,1)S(1)}, bf16[512,3072]{1,0:T(8,128)(2,1)}, u32[]{:S(2)}) copy-start(bf16[512,3072]{1,0:T(8,128)(2,1)} %get-tuple-element.27) | copy-start | bytes 9437188
  534.3 52.1 %copy-start.15 = (bf16[512,3072]{1,0:T(8,128)(2,1)S(1)}, bf16[512,3072]{1,0:T(8,128)(2,1)}, u32[]{:S(2)}) copy-start(bf16[512,3072]{1,0:T(8,128)(2,1)} %get-tuple-element.28) | copy-start | bytes 9437188
  586.0 141.3 %collective-permute-start.13 = (bf16[768,2688]{1,0:T(8,128)(2,1)}, bf16[768,2688]{1,0:T(8,128)(2,1)}, u32[]{:S(2)}, u32[]{:S(2)}) collective-permute-start(bf16[768,2688]{1,0:T(8,128)(2,1)} %collective-permute-done.8), channel_id=1, source_target_pairs={{0,8},{4,12},{8,0},{12,4},{1,9},{5,13},{9,1},{13,5},{2,10},{6,14},... | collective-permute-start | bytes 12386312 | tf_op jit(solution)/shard_map/ppermute | solution.py:211
  603.9 82.1 %collective-permute-start.14 = (bf16[768,1536]{1,0:T(8,128)(2,1)S(1)}, bf16[768,1536]{1,0:T(8,128)(2,1)S(1)}, u32[]{:S(2)}, u32[]{:S(2)}) collective-permute-start(bf16[768,1536]{1,0:T(8,128)(2,1)S(1)} %fusion.28), channel_id=1, source_target_pairs={{0,0},{1,8},{2,4},{3,12},{4,2},{5,10},{6,6},{7,14},{8,1},{9,9},{10... | collective-permute-start | bytes 7077896 | tf_op jit(solution)/shard_map/ppermute | solution.py:218
  619.8 112.4 %collective-permute-start.17 = (bf16[2,768,1152]{2,1,0:T(8,128)(2,1)}, bf16[2,768,1152]{2,1,0:T(8,128)(2,1)}, u32[]{:S(2)}, u32[]{:S(2)}) collective-permute-start(bf16[2,768,1152]{2,1,0:T(8,128)(2,1)} %dynamic-slice_bitcast_fusion.3), channel_id=1, source_target_pairs={{0,4},{4,0},{8,12},{12,8},{1,5},{5,1},{9,13},{13,9},{2,6},{6,2},{1... | collective-permute-start | bytes 10616840 | tf_op jit(solution)/shard_map/ppermute | solution.py:211
  620.2 116.9 %collective-permute-start.9 = (bf16[768,2688]{1,0:T(8,128)(2,1)}, bf16[768,2688]{1,0:T(8,128)(2,1)}, u32[]{:S(2)}, u32[]{:S(2)}) collective-permute-start(bf16[768,2688]{1,0:T(8,128)(2,1)} %collective-permute-done.8), channel_id=1, source_target_pairs={{0,4},{4,0},{8,12},{12,8},{1,5},{5,1},{9,13},{13,9},{2,6},{6,2},{1... | collective-permute-start | bytes 12386312 | tf_op jit(solution)/shard_map/ppermute | solution.py:211
  727.4 21.7 %collective-permute-start.15 = (bf16[768,2688]{1,0:T(8,128)(2,1)}, bf16[768,2688]{1,0:T(8,128)(2,1)}, u32[]{:S(2)}, u32[]{:S(2)}) collective-permute-start(bf16[768,2688]{1,0:T(8,128)(2,1)} %collective-permute-done.13), channel_id=1, source_target_pairs={{0,4},{4,0},{8,12},{12,8},{1,5},{5,1},{9,13},{13,9},{2,6},{6,2},{1... | collective-permute-start | bytes 12386312 | tf_op jit(solution)/shard_map/ppermute | solution.py:211
  743.0 41.3 %collective-permute-start.18 = (bf16[768,1152]{1,0:T(8,128)(2,1)}, bf16[768,1152]{1,0:T(8,128)(2,1)}, u32[]{:S(2)}, u32[]{:S(2)}) collective-permute-start(bf16[768,1152]{1,0:T(8,128)(2,1)} %dynamic-slice_bitcast_fusion.6), channel_id=1, source_target_pairs={{0,8},{4,12},{8,0},{12,4},{1,9},{5,13},{9,1},{13,5},{2,10},{6,14},... | collective-permute-start | bytes 5308424 | tf_op jit(solution)/shard_map/ppermute | solution.py:211
  778.4 70.8 %collective-permute-start.16 = (bf16[512,3072]{1,0:T(8,128)(2,1)}, bf16[512,3072]{1,0:T(8,128)(2,1)}, u32[]{:S(2)}, u32[]{:S(2)}) collective-permute-start(bf16[512,3072]{1,0:T(8,128)(2,1)} %add_convert_fusion.2), channel_id=1, source_target_pairs={{0,16},{16,0},{1,17},{17,1},{2,18},{18,2},{3,19},{19,3},{4,20},{20... | collective-permute-start | bytes 9437192 | tf_op jit(solution)/shard_map/ppermute | solution.py:211
  788.0 69.1 %collective-permute-start.19 = (bf16[768,1152]{1,0:T(8,128)(2,1)}, bf16[768,1152]{1,0:T(8,128)(2,1)}, u32[]{:S(2)}, u32[]{:S(2)}) collective-permute-start(bf16[768,1152]{1,0:T(8,128)(2,1)} %fusion.31), channel_id=1, source_target_pairs={{0,0},{1,8},{2,4},{3,12},{4,2},{5,10},{6,6},{7,14},{8,1},{9,9},{10... | collective-permute-start | bytes 5308424 | tf_op jit(solution)/shard_map/ppermute | solution.py:218
  857.1 62.3 %copy-start.1 = (bf16[1024,1536]{1,0:T(8,128)(2,1)S(1)}, bf16[1024,1536]{1,0:T(8,128)(2,1)}, u32[]{:S(2)}) copy-start(bf16[1024,1536]{1,0:T(8,128)(2,1)} %param.12) | copy-start | bytes 9437188
  (17 other events, 152.1 us)
Sparse Core Ops, SparseCore 0:
  79.6 64.8 all-gather.4
  260.1 60.7 all-gather.6
  857.2 57.7 reduce-scatter.1

commit v4 on v3

--- a/solution.py
+++ b/solution.py
@@ -245,8 +245,8 @@
     return add(lax.dynamic_index_in_dim(pair, row, 0, keepdims=False), arrived)
 
 
-def four_parts(block, *earlier):
-    opposite = exchange(after(block, *earlier), "gy", 2)
+def four_parts(block):
+    opposite = exchange(block, "gy", 2)
     beside = exchange(block, "gy", 1)
     return block, beside, opposite, exchange(opposite, "gy", 1)
 
@@ -278,7 +278,7 @@
 
     grad_blocks = lax.all_gather(out_grad, "gz", axis=0)
     out_block = jnp.concatenate([hidden_out, attend_out], axis=0)
-    turned_out = turn(after(out_block, grad_blocks))
+    turned_out = turn(out_block)
     grad_own = both_halves(out_grad)
     activated = gelu_value(hidden_pre.astype(jnp.float32)).astype(jnp.bfloat16)
     part_attend_out = jnp.einsum(
@@ -287,8 +287,6 @@
     part_hidden_out = jnp.einsum(
         "tg,td->gd", activated, grad_own, preferred_element_type=jnp.float32
     ).astype(jnp.bfloat16)
-    out_sum = far_sum(pair_sum([part_hidden_out, part_attend_out]))
-    hidden_out_grad, attend_out_grad = out_sum[:units], out_sum[units:]
 
     order = []
     for flip in range(4):
@@ -299,11 +297,15 @@
             [lax.dynamic_index_in_dim(grad_blocks, at, 0, keepdims=False) for at in order], axis=1
         )
     )
-    out_parts = four_parts(turned_out, out_sum, grad_slab)
-    normed_blocks = lax.all_gather(after(normed, turned_out, grad_slab), "gz", axis=0)
+    out_parts = four_parts(turned_out)
+    out_sum = far_sum(pair_sum([part_hidden_out, part_attend_out]), out_parts[2])
+    hidden_out_grad, attend_out_grad = out_sum[:units], out_sum[units:]
+    normed_blocks = lax.all_gather(after(normed, grad_blocks, part_attend_out, part_hidden_out), "gz", axis=0)
     in_block = jnp.concatenate([hidden_in, attend_in], axis=1)
     turned_in = turn(after(in_block, out_parts[2]))
-    normed_slab = both_halves(jnp.concatenate([normed_blocks[at] for at in SWAP], axis=1))
+    normed_slab = both_halves(
+        after(jnp.concatenate([normed_blocks[at] for at in SWAP], axis=1), grad_slab)
+    )
     hidden_rows = jnp.concatenate([part[:units] for part in out_parts], axis=1)
     attend_rows = jnp.concatenate([part[units:] for part in out_parts], axis=1)
 
@@ -325,15 +327,9 @@
         "td,tq->dq", normed_slab, projected_grad, preferred_element_type=jnp.float32
     ).astype(jnp.bfloat16)
 
-    hidden_in_sum = far_sum(pair_sum([part_hidden_in]))
+    hidden_in_sum = far_sum(pair_sum([part_hidden_in]), out_sum)
     hidden_in_grad = turn(hidden_in_sum)
-    far_in = exchange(after(turned_in, hidden_in_sum), "gy", 2)
-    in_parts = (
-        turned_in,
-        exchange(turned_in, "gy", 1),
-        far_in,
-        exchange(after(far_in, hidden_in_grad), "gy", 1),
-    )
+    in_parts = four_parts(turned_in)
     attend_in_sum = far_sum(pair_sum([part_attend_in]), in_parts[2])
     attend_in_grad = turn(attend_in_sum)
     hidden_cols = jnp.concatenate([part[:, :units] for part in in_parts], axis=0)
@@ -359,7 +355,7 @@
         axis=1,
     )
     normed_grad = lax.psum_scatter(
-        after(row_grad, attend_in_grad), "gz", scatter_dimension=1, tiled=True
+        after(row_grad, hidden_in_grad), "gz", scatter_dimension=1, tiled=True
     )
     return normed_grad, attend_in_grad, hidden_in_grad, attend_out_grad, hidden_out_grad
 

time: 942 us -> 846 us (0.90)
  waiting for transfers between devices: 593 us -> 520 us
  starting transfers between devices: 35.6 us -> 18 us
    ppermute x16, waiting for transfers between devices: 317 us -> 173 us  [exchange(): return lax.ppermute(block, axis, [(i, i ^ flip) for i in range(size)])]
    ppermute x4, waiting for transfers between devices: 158 us -> 275 us  [turn(): return lax.ppermute(block, ('gy', 'gz'), pairs)]
    reduce_scatter x1, waiting for transfers between devices: 52.5 us -> 0.01 us  [local_columns(): lax.psum_scatter(after(row_grad, hidden_in_grad), 'gz', scatter_dimension...]
    ppermute x16, starting transfers between devices: 27.3 us -> 7.87 us  [exchange(): return lax.ppermute(block, axis, [(i, i ^ flip) for i in range(size)])]
  transfers between devices with their start and end apart: 23 -> 23, of which waited for: 15 -> 11; matrix products, arithmetic and copies ran while one was open for 20% -> 30% of each run, Pallas kernels for 2% -> 2%
where the time goes in v4:
time: 846 us; the launch traced here: 836 us
  waiting for transfers between devices  520 us (61%)
  matrix products  114 us (13%)
  local copies, waits for them, and re-layouts  103 us (12%)
  other arithmetic  53.1 us (6%)
  starting transfers between devices  18 us (2%)
  between operations  14.4 us (2%)
  Pallas kernels  14.1 us (2%)
    ppermute x4, waiting for transfers between devices, turn(): return lax.ppermute(block, ('gy', 'gz'), pairs)  275 us
    ppermute x16, waiting for transfers between devices, exchange(): return lax.ppermute(block, axis, [(i, i ^ flip) for i in range(size)])  173 us
    all_gather x1, waiting for transfers between devices, local_columns(): grad_blocks = lax.all_gather(out_grad, 'gz', axis=0)  71.3 us
    dot_general x2, matrix products, input_grad(): jnp.einsum('tq,dq->td', hidden_part, hidden_cols, preferred_element_type=...  25.9 us
    dot_general x2, matrix products, input_grad(): jnp.einsum('tq,dq->td', attend_part, attend_cols, preferred_element_type=...  22.6 us
    convert_element_type x6, other arithmetic, add(): (left.astype(jnp.float32) + right.astype(jnp.float32)).astype(jnp.bfloat16)  21.7 us
    dot_general x1, matrix products, local_columns(): jnp.einsum('td,gd->tg', grad_slab, hidden_rows, preferred_element_type=jn...  17.4 us
    dynamic_slice x3, local copies, waits for them, and re-layouts, at_place(): lax.dynamic_index_in_dim(part, index, axis, keepdims=False)  17.3 us
  transfers between devices with their start and end apart: 23, of which 11 were waited for; matrix products, arithmetic and copies ran while one was open for 30% of the time, Pallas kernels for 2%

profile of v4, /device:TPU:4, one launch (start us, length us, event | category | flops | bytes accessed | tf_op | source)
XLA Modules:
  0.0 836.0 jit_solution(15199303191221465752)
XLA Ops:
  16.6 11.1 %collective-permute-done.10 = bf16[512,768]{1,0:T(8,128)(2,1)} collective-permute-done((bf16[512,768]{1,0:T(8,128)(2,1)}, bf16[512,768]{1,0:T(8,128)(2,1)}, u32[]{:S(2)}, u32[]{:S(2)}) %collective-permute-start.10) | collective-permute-done | bytes 786464 | tf_op jit(solution)/shard_map/ppermute | solution.py:211
  33.0 16.5 %fusion.6 = bf16[6144,768]{1,0:T(8,128)(2,1)} fusion(bf16[1024,6144]{1,0:T(8,128)(2,1)} %param.13, bf16[512,768]{1,0:T(8,128)(2,1)S(1)} %get-tuple-element.42, bf16[512,768]{1,0:T(8,128)(2,1)S(1)} %get-tuple-element.41), kind=kOutput, calls=%fused_computation.14 | convolution fusion | flops 9709289472 | bytes 23592960 | tf_op jit(solution)/shard_map/tg,td->gd/dot_general | solution.py:287
  49.5 71.3 %all-gather.5.cloned.1.call-done = bf16[2048,768]{1,0:T(8,128)(2,1)} async-done(((bf16[512,768]{1,0:T(8,128)(2,1)}), bf16[2048,768]{1,0:T(8,128)(2,1)}) %all-gather.5.cloned.1.call-update) | async-done | bytes 3145744 | tf_op jit(solution)/shard_map/all_gather | solution.py:279
  121.4 70.9 %collective-permute-done.1 = bf16[1920,768]{1,0:T(8,128)(2,1)} collective-permute-done((bf16[1920,768]{1,0:T(8,128)(2,1)}, bf16[1920,768]{1,0:T(8,128)(2,1)}, u32[]{:S(2)}, u32[]{:S(2)}) %collective-permute-start.1) | collective-permute-done | bytes 2949152 | tf_op jit(solution)/shard_map/ppermute | solution.py:218
  196.7 4.5 pad_maximum_fusion.5
  201.2 4.9 reshape.34
  206.1 21.9 %collective-permute-done.3 = bf16[1920,768]{1,0:T(8,128)(2,1)} collective-permute-done((bf16[1920,768]{1,0:T(8,128)(2,1)}, bf16[1920,768]{1,0:T(8,128)(2,1)}, u32[]{:S(2)}, u32[]{:S(2)}) %collective-permute-start.3) | collective-permute-done | bytes 2949152 | tf_op jit(solution)/shard_map/ppermute | solution.py:211
  228.0 7.0 constant_dynamic-slice_fusion.1
  235.0 5.4 copy.16
  240.4 6.6 dynamic-slice_bitcast_fusion.1
  268.2 4.7 broadcast_select_fusion.3
  276.1 17.4 %fusion.26 = bf16[1024,1536]{1,0:T(8,128)(2,1)} fusion(bf16[1536,768]{1,0:T(8,128)(2,1)} %slice.103, bf16[1536,768]{1,0:T(8,128)(2,1)} %slice.102, bf16[1536,768]{1,0:T(8,128)(2,1)} %slice.101, bf16[1536,768]{1,0:T(8,128)(2,1)} %slice.100, bf16[1024,6144]{1,0:T(8,128)(2,1)} %param.13, s32[]{:T(128)S(6)} %select_n.134, ...), kind=kOutput, calls=%fused_computation.40 | convolution fusion | flops 9731309568 | bytes 22020100 | tf_op jit(solution)/shard_map/td,gd->tg/dot_general | solution.py:313
  293.5 92.3 %collective-permute-done.5 = bf16[768,2688]{1,0:T(8,128)(2,1)} collective-permute-done((bf16[768,2688]{1,0:T(8,128)(2,1)}, bf16[768,2688]{1,0:T(8,128)(2,1)}, u32[]{:S(2)}, u32[]{:S(2)}) %collective-permute-start.5) | collective-permute-done | bytes 4128800 | tf_op jit(solution)/shard_map/ppermute | solution.py:218
  385.8 4.0 broadcast_select_fusion.1
  389.8 13.8 %convolution_convert_fusion.1 = bf16[3072,1536]{1,0:T(8,128)(2,1)S(1)} fusion(bf16[1024,1536]{1,0:T(8,128)(2,1)} %fusion.26, bf16[512,3072]{1,0:T(8,128)(2,1)} %get-tuple-element.24, bf16[512,3072]{1,0:T(8,128)(2,1)S(1)} %get-tuple-element.23), kind=kOutput, calls=%fused_computation.9 | convolution fusion | flops 9680977920 | bytes 18874368 | tf_op jit(solution)/shard_map/td,tq->dq/dot_general | solution.py:317
  409.0 4.8 copy.15
  414.3 5.7 add_convert_fusion
  426.3 51.9 %collective-permute-done.7 = bf16[768,2688]{1,0:T(8,128)(2,1)} collective-permute-done((bf16[768,2688]{1,0:T(8,128)(2,1)}, bf16[768,2688]{1,0:T(8,128)(2,1)}, u32[]{:S(2)}, u32[]{:S(2)}) %collective-permute-start.7) | collective-permute-done | bytes 4128800 | tf_op jit(solution)/shard_map/ppermute | solution.py:211
  488.8 14.1 %shard_map.128 = bf16[1024,1152]{1,0:T(8,128)(2,1)S(1)} custom-call(bf16[1024,1152]{1,0:T(8,128)(2,1)S(1)} %constant_dynamic-slice_fusion.6.keyed_ref, bf16[1024,384]{1,0:T(8,128)(2,1)S(1)} %fusion.45.grad_ref), custom_call_target="tpu_custom_call" | custom-call | flops 4026531840 | bytes 5505024 | tf_op jit(solution)/shard_map/pallas_call | solution.py:191
  502.9 34.4 %collective-permute-done.14 = bf16[1920,768]{1,0:T(8,128)(2,1)} collective-permute-done((bf16[1920,768]{1,0:T(8,128)(2,1)}, bf16[1920,768]{1,0:T(8,128)(2,1)}, u32[]{:S(2)}, u32[]{:S(2)}) %collective-permute-start.14) | collective-permute-done | bytes 2949152 | tf_op jit(solution)/shard_map/ppermute | solution.py:211
  537.4 4.2 fusion.27
  567.4 13.2 %fusion.41 = f32[512,3072]{1,0:T(8,128)} fusion(bf16[768,1536]{1,0:T(8,128)(2,1)} %slice.107, bf16[768,1536]{1,0:T(8,128)(2,1)} %slice.106, bf16[768,1536]{1,0:T(8,128)(2,1)} %slice.105, bf16[768,1536]{1,0:T(8,128)(2,1)} %slice.104, bf16[1024,1536]{1,0:T(8,128)(2,1)} %fusion.26, s32[]{:T(128)S(6)} %select_n.135), kind=kOutput, calls=%fused_computation.74 | convolution fusion | flops 4869586944 | bytes 17301508 | tf_op jit(solution)/shard_map/tq,dq->td/dot_general | solution.py:343
  583.4 10.8 %add_convert_fusion.2 = bf16[512,3072]{1,0:T(8,128)(2,1)} fusion(f32[512,3072]{1,0:T(8,128)} %fusion.41, bf16[768,1152]{1,0:T(8,128)(2,1)} %slice.99, bf16[768,1152]{1,0:T(8,128)(2,1)} %slice.98, bf16[768,1152]{1,0:T(8,128)(2,1)} %slice.97, bf16[768,1152]{1,0:T(8,128)(2,1)S(1)} %slice.96, bf16[1024,1152]{1,0:T(8,128)(2,1)S(1)} %shard_map.128, s32[]{:T(128)S(6)} %select_n.135), kind=kOutput, calls=%fused_computation.39 | convolution fusion | flops 3655335936 | bytes 17694724 | tf_op jit(solution)/shard_map/tq,dq->td/dot_general | solution.py:341
  594.6 10.2 %convolution_convert_fusion = bf16[3072,1152]{1,0:T(8,128)(2,1)S(1)} fusion(bf16[1024,1152]{1,0:T(8,128)(2,1)S(1)} %shard_map.128, bf16[512,3072]{1,0:T(8,128)(2,1)} %get-tuple-element.24, bf16[512,3072]{1,0:T(8,128)(2,1)S(1)} %copy-done.17), kind=kOutput, calls=%fused_computation.8 | convolution fusion | flops 7263879168 | bytes 15728640 | tf_op jit(solution)/shard_map/td,tq->dq/dot_general | solution.py:326
  609.8 12.7 %fusion.42 = f32[512,3072]{1,0:T(8,128)} fusion(bf16[768,1536]{1,0:T(8,128)(2,1)} %slice.107, bf16[768,1536]{1,0:T(8,128)(2,1)} %slice.106, bf16[768,1536]{1,0:T(8,128)(2,1)} %slice.105, bf16[768,1536]{1,0:T(8,128)(2,1)} %slice.104, bf16[1024,1536]{1,0:T(8,128)(2,1)} %fusion.26, s32[]{:T(128)S(6)} %select_n.133), kind=kOutput, calls=%fused_computation.75 | convolution fusion | flops 4869586944 | bytes 17301508 | tf_op jit(solution)/shard_map/tq,dq->td/dot_general | solution.py:343
  628.7 11.8 %fusion.48 = f32[512,3072]{1,0:T(8,128)} fusion(bf16[768,1152]{1,0:T(8,128)(2,1)S(1)} %copy-done.22, bf16[768,1152]{1,0:T(8,128)(2,1)S(1)} %copy-done.20, bf16[768,1152]{1,0:T(8,128)(2,1)S(1)} %copy-done.21, bf16[768,1152]{1,0:T(8,128)(2,1)S(1)} %slice.96, bf16[1024,1152]{1,0:T(8,128)(2,1)S(1)} %shard_map.128, s32[]{:T(128)S(6)} %select_n.133), kind=kOutput, calls=%fused_computation.80 | convolution fusion | flops 3652190208 | bytes 14548996 | tf_op jit(solution)/shard_map/tq,dq->td/dot_general | solution.py:341
  640.5 20.0 %collective-permute-done.9 = bf16[512,3072]{1,0:T(8,128)(2,1)} collective-permute-done((bf16[512,3072]{1,0:T(8,128)(2,1)}, bf16[512,3072]{1,0:T(8,128)(2,1)}, u32[]{:S(2)}, u32[]{:S(2)}) %collective-permute-start.9) | collective-permute-done | bytes 3145760 | tf_op jit(solution)/shard_map/ppermute | solution.py:211
  660.6 5.5 add_convert_fusion.1
  668.4 40.8 %collective-permute-done.16 = bf16[768,1536]{1,0:T(8,128)(2,1)} collective-permute-done((bf16[768,1536]{1,0:T(8,128)(2,1)}, bf16[768,1536]{1,0:T(8,128)(2,1)}, u32[]{:S(2)}, u32[]{:S(2)}) %collective-permute-start.16) | collective-permute-done | bytes 2359328 | tf_op jit(solution)/shard_map/ppermute | solution.py:218
  709.3 3.9 fusion.18
  713.5 33.5 %collective-permute-done.18 = bf16[768,1152]{1,0:T(8,128)(2,1)S(1)} collective-permute-done((bf16[768,1152]{1,0:T(8,128)(2,1)S(1)}, bf16[768,1152]{1,0:T(8,128)(2,1)S(1)}, u32[]{:S(2)}, u32[]{:S(2)}) %collective-permute-start.18) | collective-permute-done | bytes 1769504 | tf_op jit(solution)/shard_map/ppermute | solution.py:211
  751.8 71.5 %collective-permute-done.19 = bf16[768,1152]{1,0:T(8,128)(2,1)} collective-permute-done((bf16[768,1152]{1,0:T(8,128)(2,1)S(1)}, bf16[768,1152]{1,0:T(8,128)(2,1)}, u32[]{:S(2)}, u32[]{:S(2)}) %collective-permute-start.19) | collective-permute-done | bytes 1769504 | tf_op jit(solution)/shard_map/ppermute | solution.py:218
  (136 shorter events, 120.4 us)
Async XLA Ops:
  7.2 21.9 %copy-start = (bf16[1024,1536]{1,0:T(8,128)(2,1)S(1)}, bf16[1024,1536]{1,0:T(8,128)(2,1)}, u32[]{:S(2)}) copy-start(bf16[1024,1536]{1,0:T(8,128)(2,1)} %param.12) | copy-start | bytes 9437188
  7.2 113.6 %all-gather.5.cloned.1.call-start = ((), (), s32[]{:S(2)}) async-start(), calls=%async_computation.2 | async-start | bytes 3932160 | tf_op jit(solution)/shard_map/all_gather | solution.py:279
  7.9 256.3 %all-gather.7.cloned.1.call-start = ((), (), s32[]{:S(2)}) async-start(), calls=%async_computation.3 | async-start | bytes 3932160 | tf_op jit(solution)/shard_map/all_gather | solution.py:303
  8.0 19.7 %collective-permute-start.10 = (bf16[512,768]{1,0:T(8,128)(2,1)}, bf16[512,768]{1,0:T(8,128)(2,1)}, u32[]{:S(2)}, u32[]{:S(2)}) collective-permute-start(bf16[512,768]{1,0:T(8,128)(2,1)} %param.10), channel_id=1, source_target_pairs={{0,16},{16,0},{1,17},{17,1},{2,18},{18,2},{3,19},{19,3},{4,20},{20... | collective-permute-start | bytes 2359304 | tf_op jit(solution)/shard_map/ppermute | solution.py:211
  13.1 179.1 %collective-permute-start.1 = (bf16[1920,768]{1,0:T(8,128)(2,1)}, bf16[1920,768]{1,0:T(8,128)(2,1)}, u32[]{:S(2)}, u32[]{:S(2)}) collective-permute-start(bf16[1920,768]{1,0:T(8,128)(2,1)} %pad_maximum_fusion.11), channel_id=1, source_target_pairs={{0,0},{1,8},{2,4},{3,12},{4,2},{5,10},{6,6},{7,14},{8,1},{9,9},{10... | collective-permute-start | bytes 8847368 | tf_op jit(solution)/shard_map/ppermute | solution.py:218
  120.8 702.4 %reduce-scatter.2.cloned.1.call-start = ((), (), s32[]{:S(2)}) async-start(), calls=%async_computation.1 | async-start | bytes 3932160 | tf_op jit(solution)/shard_map/reduce_scatter | solution.py:357
  192.2 35.8 %collective-permute-start.3 = (bf16[1920,768]{1,0:T(8,128)(2,1)}, bf16[1920,768]{1,0:T(8,128)(2,1)}, u32[]{:S(2)}, u32[]{:S(2)}) collective-permute-start(bf16[1920,768]{1,0:T(8,128)(2,1)} %collective-permute-done.1), channel_id=1, source_target_pairs={{0,8},{4,12},{8,0},{12,4},{1,9},{5,13},{9,1},{13,5},{2,10},{6,14},... | collective-permute-start | bytes 8847368 | tf_op jit(solution)/shard_map/ppermute | solution.py:211
  192.2 68.8 %collective-permute-start.2 = (bf16[1920,768]{1,0:T(8,128)(2,1)}, bf16[1920,768]{1,0:T(8,128)(2,1)}, u32[]{:S(2)}, u32[]{:S(2)}) collective-permute-start(bf16[1920,768]{1,0:T(8,128)(2,1)} %collective-permute-done.1), channel_id=1, source_target_pairs={{0,4},{4,0},{8,12},{12,8},{1,5},{5,1},{9,13},{13,9},{2,6},{6,2},{1... | collective-permute-start | bytes 8847368 | tf_op jit(solution)/shard_map/ppermute | solution.py:211
  196.4 71.2 %collective-permute-start = (bf16[512,3072]{1,0:T(8,128)(2,1)}, bf16[512,3072]{1,0:T(8,128)(2,1)}, u32[]{:S(2)}, u32[]{:S(2)}) collective-permute-start(bf16[512,3072]{1,0:T(8,128)(2,1)} %pad_maximum_fusion.8), channel_id=1, source_target_pairs={{0,16},{16,0},{1,17},{17,1},{2,18},{18,2},{3,19},{19,3},{4,20},{20... | collective-permute-start | bytes 9437192 | tf_op jit(solution)/shard_map/ppermute | solution.py:211
  228.0 44.9 %collective-permute-start.4 = (bf16[1920,768]{1,0:T(8,128)(2,1)}, bf16[1920,768]{1,0:T(8,128)(2,1)}, u32[]{:S(2)}, u32[]{:S(2)}) collective-permute-start(bf16[1920,768]{1,0:T(8,128)(2,1)} %collective-permute-done.3), channel_id=1, source_target_pairs={{0,4},{4,0},{8,12},{12,8},{1,5},{5,1},{9,13},{13,9},{2,6},{6,2},{1... | collective-permute-start | bytes 8847368 | tf_op jit(solution)/shard_map/ppermute | solution.py:211
  247.0 138.7 %collective-permute-start.5 = (bf16[768,2688]{1,0:T(8,128)(2,1)}, bf16[768,2688]{1,0:T(8,128)(2,1)}, u32[]{:S(2)}, u32[]{:S(2)}) collective-permute-start(bf16[768,2688]{1,0:T(8,128)(2,1)} %pad_maximum_fusion.5), channel_id=1, source_target_pairs={{0,0},{1,8},{2,4},{3,12},{4,2},{5,10},{6,6},{7,14},{8,1},{9,9},{10... | collective-permute-start | bytes 12386312 | tf_op jit(solution)/shard_map/ppermute | solution.py:218
  251.8 162.5 %collective-permute-start.13 = (bf16[2,1920,768]{2,1,0:T(8,128)(2,1)}, bf16[2,1920,768]{2,1,0:T(8,128)(2,1)}, u32[]{:S(2)}, u32[]{:S(2)}) collective-permute-start(bf16[2,1920,768]{2,1,0:T(8,128)(2,1)} %pad_maximum_fusion.4), channel_id=1, source_target_pairs={{0,4},{4,0},{8,12},{12,8},{1,5},{5,1},{9,13},{13,9},{2,6},{6,2},{1... | collective-permute-start | bytes 17694728 | tf_op jit(solution)/shard_map/ppermute | solution.py:211
  266.9 118.8 %collective-permute-start.11 = (bf16[512,3072]{1,0:T(8,128)(2,1)S(1)}, bf16[512,3072]{1,0:T(8,128)(2,1)}, u32[]{:S(2)}, u32[]{:S(2)}) collective-permute-start(bf16[512,3072]{1,0:T(8,128)(2,1)S(1)} %pad_maximum_fusion.10), channel_id=1, source_target_pairs={{0,16},{16,0},{1,17},{17,1},{2,18},{18,2},{3,19},{19,3},{4,20},{20... | collective-permute-start | bytes 9437192 | tf_op jit(solution)/shard_map/ppermute | solution.py:211
  385.8 92.4 %collective-permute-start.7 = (bf16[768,2688]{1,0:T(8,128)(2,1)}, bf16[768,2688]{1,0:T(8,128)(2,1)}, u32[]{:S(2)}, u32[]{:S(2)}) collective-permute-start(bf16[768,2688]{1,0:T(8,128)(2,1)} %collective-permute-done.5), channel_id=1, source_target_pairs={{0,8},{4,12},{8,0},{12,4},{1,9},{5,13},{9,1},{13,5},{2,10},{6,14},... | collective-permute-start | bytes 12386312 | tf_op jit(solution)/shard_map/ppermute | solution.py:211
  389.8 13.8 %copy-start.16 = (bf16[512,3072]{1,0:T(8,128)(2,1)}, bf16[512,3072]{1,0:T(8,128)(2,1)S(1)}, u32[]{:S(2)}) copy-start(bf16[512,3072]{1,0:T(8,128)(2,1)S(1)} %get-tuple-element.23) | copy-start | bytes 9437188
  409.0 150.0 %collective-permute-start.12 = (bf16[2,768,1536]{2,1,0:T(8,128)(2,1)}, bf16[2,768,1536]{2,1,0:T(8,128)(2,1)}, u32[]{:S(2)}, u32[]{:S(2)}) collective-permute-start(bf16[2,768,1536]{2,1,0:T(8,128)(2,1)} %dynamic-slice_bitcast_fusion.2), channel_id=1, source_target_pairs={{0,4},{4,0},{8,12},{12,8},{1,5},{5,1},{9,13},{13,9},{2,6},{6,2},{1... | collective-permute-start | bytes 14155784 | tf_op jit(solution)/shard_map/ppermute | solution.py:211
  413.8 139.0 %collective-permute-start.6 = (bf16[768,2688]{1,0:T(8,128)(2,1)}, bf16[768,2688]{1,0:T(8,128)(2,1)}, u32[]{:S(2)}, u32[]{:S(2)}) collective-permute-start(bf16[768,2688]{1,0:T(8,128)(2,1)} %collective-permute-done.5), channel_id=1, source_target_pairs={{0,4},{4,0},{8,12},{12,8},{1,5},{5,1},{9,13},{13,9},{2,6},{6,2},{1... | collective-permute-start | bytes 12386312 | tf_op jit(solution)/shard_map/ppermute | solution.py:211
  424.3 113.1 %collective-permute-start.14 = (bf16[1920,768]{1,0:T(8,128)(2,1)}, bf16[1920,768]{1,0:T(8,128)(2,1)}, u32[]{:S(2)}, u32[]{:S(2)}) collective-permute-start(bf16[1920,768]{1,0:T(8,128)(2,1)} %dynamic-slice_bitcast_fusion.4), channel_id=1, source_target_pairs={{0,8},{4,12},{8,0},{12,4},{1,9},{5,13},{9,1},{13,5},{2,10},{6,14},... | collective-permute-start | bytes 8847368 | tf_op jit(solution)/shard_map/ppermute | solution.py:211
  478.2 86.0 %collective-permute-start.8 = (bf16[768,2688]{1,0:T(8,128)(2,1)}, bf16[768,2688]{1,0:T(8,128)(2,1)}, u32[]{:S(2)}, u32[]{:S(2)}) collective-permute-start(bf16[768,2688]{1,0:T(8,128)(2,1)} %collective-permute-done.7), channel_id=1, source_target_pairs={{0,4},{4,0},{8,12},{12,8},{1,5},{5,1},{9,13},{13,9},{2,6},{6,2},{1... | collective-permute-start | bytes 12386312 | tf_op jit(solution)/shard_map/ppermute | solution.py:211
  484.1 53.3 %slice-start = ((s8[5898240]{0:T(1024)(128)(4,1)}), s8[4194304]{0:T(1024)(128)(4,1)S(1)}, s32[]{:S(2)}) async-start(s8[5898240]{0:T(1024)(128)(4,1)} %bitcast.54), calls=%async_computation.4 | async-start | bytes 8388608
  485.4 52.0 %slice-start.1 = ((s8[5898240]{0:T(1024)(128)(4,1)}), s8[1703936]{0:T(1024)(128)(4,1)S(1)}, s32[]{:S(2)}) async-start(s8[5898240]{0:T(1024)(128)(4,1)} %bitcast.54), calls=%async_computation.5 | async-start | bytes 3407872
  543.2 15.8 %slice-start.2 = ((s8[9437184]{0:T(1024)(128)(4,1)}), s8[4194304]{0:T(1024)(128)(4,1)S(1)}, s32[]{:S(2)}) async-start(s8[9437184]{0:T(1024)(128)(4,1)} %bitcast.58), calls=%async_computation.6 | async-start | bytes 8388608
  546.6 12.4 %slice-start.3 = ((s8[9437184]{0:T(1024)(128)(4,1)}), s8[4194304]{0:T(1024)(128)(4,1)S(1)}, s32[]{:S(2)}) async-start(s8[9437184]{0:T(1024)(128)(4,1)} %bitcast.58), calls=%async_computation.7 | async-start | bytes 8388608
  564.2 58.3 %collective-permute-start.15 = (bf16[768,1536]{1,0:T(8,128)(2,1)}, bf16[768,1536]{1,0:T(8,128)(2,1)}, u32[]{:S(2)}, u32[]{:S(2)}) collective-permute-start(bf16[768,1536]{1,0:T(8,128)(2,1)} %dynamic-slice_bitcast_fusion.5), channel_id=1, source_target_pairs={{0,8},{4,12},{8,0},{12,4},{1,9},{5,13},{9,1},{13,5},{2,10},{6,14},... | collective-permute-start | bytes 7077896 | tf_op jit(solution)/shard_map/ppermute | solution.py:211
  594.2 66.4 %collective-permute-start.9 = (bf16[512,3072]{1,0:T(8,128)(2,1)}, bf16[512,3072]{1,0:T(8,128)(2,1)}, u32[]{:S(2)}, u32[]{:S(2)}) collective-permute-start(bf16[512,3072]{1,0:T(8,128)(2,1)} %add_convert_fusion.2), channel_id=1, source_target_pairs={{0,16},{16,0},{1,17},{17,1},{2,18},{18,2},{3,19},{19,3},{4,20},{20... | collective-permute-start | bytes 9437192 | tf_op jit(solution)/shard_map/ppermute | solution.py:211
  609.8 99.5 %collective-permute-start.17 = (bf16[2,768,1152]{2,1,0:T(8,128)(2,1)}, bf16[2,768,1152]{2,1,0:T(8,128)(2,1)}, u32[]{:S(2)}, u32[]{:S(2)}) collective-permute-start(bf16[2,768,1152]{2,1,0:T(8,128)(2,1)} %dynamic-slice_bitcast_fusion.3), channel_id=1, source_target_pairs={{0,4},{4,0},{8,12},{12,8},{1,5},{5,1},{9,13},{13,9},{2,6},{6,2},{1... | collective-permute-start | bytes 10616840 | tf_op jit(solution)/shard_map/ppermute | solution.py:211
  626.4 34.2 %copy-start.15 = (f32[512,3072]{1,0:T(8,128)S(1)}, f32[512,3072]{1,0:T(8,128)}, u32[]{:S(2)}) copy-start(f32[512,3072]{1,0:T(8,128)} %fusion.42) | copy-start | bytes 18874372
  626.4 82.9 %collective-permute-start.16 = (bf16[768,1536]{1,0:T(8,128)(2,1)}, bf16[768,1536]{1,0:T(8,128)(2,1)}, u32[]{:S(2)}, u32[]{:S(2)}) collective-permute-start(bf16[768,1536]{1,0:T(8,128)(2,1)} %fusion.28), channel_id=1, source_target_pairs={{0,0},{1,8},{2,4},{3,12},{4,2},{5,10},{6,6},{7,14},{8,1},{9,9},{10... | collective-permute-start | bytes 7077896 | tf_op jit(solution)/shard_map/ppermute | solution.py:218
  713.2 36.1 %copy-start.3 = (bf16[1920,768]{1,0:T(8,128)(2,1)S(1)}, bf16[1920,768]{1,0:T(8,128)(2,1)}, u32[]{:S(2)}) copy-start(bf16[1920,768]{1,0:T(8,128)(2,1)} %fusion.27) | copy-start | bytes 8847364
  713.4 33.6 %collective-permute-start.18 = (bf16[768,1152]{1,0:T(8,128)(2,1)S(1)}, bf16[768,1152]{1,0:T(8,128)(2,1)S(1)}, u32[]{:S(2)}, u32[]{:S(2)}) collective-permute-start(bf16[768,1152]{1,0:T(8,128)(2,1)S(1)} %dynamic-slice_bitcast_fusion.6), channel_id=1, source_target_pairs={{0,8},{4,12},{8,0},{12,4},{1,9},{5,13},{9,1},{13,5},{2,10},{6,14},... | collective-permute-start | bytes 5308424 | tf_op jit(solution)/shard_map/ppermute | solution.py:211
  747.4 75.9 %collective-permute-start.19 = (bf16[768,1152]{1,0:T(8,128)(2,1)S(1)}, bf16[768,1152]{1,0:T(8,128)(2,1)}, u32[]{:S(2)}, u32[]{:S(2)}) collective-permute-start(bf16[768,1152]{1,0:T(8,128)(2,1)S(1)} %fusion.31), channel_id=1, source_target_pairs={{0,0},{1,8},{2,4},{3,12},{4,2},{5,10},{6,6},{7,14},{8,1},{9,9},{10... | collective-permute-start | bytes 5308424 | tf_op jit(solution)/shard_map/ppermute | solution.py:218
  750.2 79.1 %copy-start.1 = (bf16[1024,1536]{1,0:T(8,128)(2,1)S(1)}, bf16[1024,1536]{1,0:T(8,128)(2,1)}, u32[]{:S(2)}) copy-start(bf16[1024,1536]{1,0:T(8,128)(2,1)} %param.12) | copy-start | bytes 9437188
  (19 other events, 85.9 us)
Sparse Core Ops, SparseCore 0:
  9.6 111.1 all-gather.4
  122.4 88.9 all-gather.6
  709.4 75.4 reduce-scatter.1
